TPU v7x, 32 devices: a whole 2x2x4 slice. The times are simulated.
32 devices in a mesh: lat: 8 (over y, x, core), lon: 4 (over z).
Axes of the slice: x: 2, y: 2, z: 4, core: 2. Of those that a mesh axis runs over, the one named last changes fastest.
Arguments:
- tokens: bfloat16 [2, 96, 96, 512], P(None, 'lat', 'lon'), may hold values from -48 to 48
- region_ids: int32 [2, 96, 96], replicated, may hold values from 0 to 3
- shifts: int32 [2], replicated, may hold values from 1 to 5, as said below
- fine_qkv: bfloat16 [512, 1536], replicated, may hold values from -2 to 2
- fine_proj: bfloat16 [512, 512], replicated, may hold values from -0.25 to 0.25
- merge_weight: bfloat16 [2048, 1024], replicated, may hold values from -0.125 to 0.125
- coarse_qkv: bfloat16 [1024, 1536], replicated, may hold values from -0.1875 to 0.1875
- coarse_proj: bfloat16 [512, 1024], replicated, may hold values from -0.25 to 0.25
Outputs:
- fine_out: bfloat16 [2, 96, 96, 512], P(None, 'lat', 'lon')
- coarse_out: bfloat16 [2, 48, 48, 1024], P(None, 'lat', 'lon')
Inputs may be any that keep to these rules, and one draw needn't show every extreme that they name: `shifts`: entry 0 is the fine level's shift, entry 1 the coarse level's; one of them is 5.
All inputs are finite; a program needn't handle non-finite values.
Results may differ from a plain program's by a relative error of at most 0.012.
The roundings to bfloat16 on the way count: a program that leaves them out, or rounds other values in their place, can miss the bound.
Values may be sent and summed in bfloat16 or wider, within the bound.
No kernel may reach another device: no remote copies, remote signals or barrier semaphores. Data moves between devices by JAX's collectives and lax.ppermute only.
A program may use at most 128 MiB of HBM per device.

v0:
```python
import functools

import jax
import jax.numpy as jnp
import numpy as np
from jax import lax
from jax.experimental import pallas as pl
from jax.experimental.pallas import tpu as pltpu
from jax.sharding import PartitionSpec as P

HD = 32
WH = 6
WW = 12
TOK = 2 * WH * WW
EPS = 1e-05
BIG = 1e30
SCALE = float(np.log2(np.e) / np.sqrt(HD))

NT = (((1,), (1,)), ((), ()))
F32 = jnp.float32
BF16 = jnp.bfloat16
I32 = jnp.int32

PAIRS = [(WH - 1, t) for t in range(1, WH)] + [(t, WH - 1) for t in range(1, WH - 1)]


def up16(count):
    return -(-count // 16) * 16


def natural(rows, cols):
    return [(l, r, c) for l in range(2) for r in range(rows) for c in range(cols)]


def windowed(rows, cols):
    return [
        (l, wr * WH + r, wc * WW + c)
        for wr in range(rows // WH)
        for wc in range(cols // WW)
        for l in range(2)
        for r in range(WH)
        for c in range(WW)
    ]


def moved(order, d):
    return [(l, r + d, c + 2 * d) for l, r, c in order]


def exchange_places(held, wanted, rows, cols, sign):
    at = {place: n for n, place in enumerate(held)}
    found = []
    for dr, dc in ((sign, 0), (0, sign), (sign, sign)):
        numbers, places = [], []
        for l, r, c in sorted(set(wanted) - set(held)):
            n = at.get((l, r - dr * rows, c - dc * cols))
            if n is not None:
                numbers.append(n)
                places.append((l, r, c))
        found.append((numbers, places))
    return found


def offsets(t0, t1):
    a = t0 if t0 <= 2 else t0 - WH
    big_a = t1 if t1 <= 2 else t1 - WH
    ahead = 1 if 2 * big_a > a or 2 * big_a - a == 0 and a < 0 else -1
    return a, big_a, ahead


def classes_of(needs, slack):
    rounded = [tuple(-(-size // 8) * 8 for size in need) for need in needs]
    heavy = [sum(need[1:3]) * 2 + sum(need[4:]) for need in rounded]
    limits = []
    for size in sorted(set(heavy)):
        if not limits or size > limits[-1][0] * slack:
            limits.append([size, size])
        limits[-1][1] = size
    which = [next(n for n, limit in enumerate(limits) if size <= limit[1]) for size in heavy]
    sizes = [
        [max(need[k] for need, w in zip(rounded, which) if w == n) for k in range(len(needs[0]))]
        for n in range(len(limits))
    ]
    return sizes, which


def rooms(sizes):
    return [up16(max(size[k] for size in sizes)) for k in range(len(sizes[0]))]


class Plan:
    def __init__(self, rows, cols):
        crows, ccols = rows // 2, cols // 2
        block, cblock = natural(rows, cols), natural(crows, ccols)
        cases = []
        for t0, t1 in PAIRS:
            a, big_a, ahead = offsets(t0, t1)
            fine = moved(windowed(rows, cols), a)
            coarse = moved(cblock, big_a)
            quarters = [
                (l, 2 * r + dr, 2 * c + dc)
                for dr, dc in ((0, 0), (1, 0), (0, 1), (1, 1))
                for l, r, c in coarse
            ]
            come = 1 if a > 0 else -1
            one = exchange_places(block, fine, rows, cols, come)
            home = [p for p in block if p not in set(fine)]
            wanted = quarters + (home if come == -ahead else [])
            two = exchange_places(fine, wanted, rows, cols, ahead)
            back = 1 if big_a < 0 else -1
            three = exchange_places(coarse, cblock, crows, ccols, back)
            got = set(fine).union(*[places for _, places in two])
            four = exchange_places(fine, [p for p in block if p not in got], rows, cols, back)
            cases.append((come, ahead, back, fine, coarse, quarters, one, two, three, four))

        def needs(which):
            return [[len(numbers) for numbers, _ in case[which]] for case in cases]

        self.one, one_class = classes_of(needs(6), 1.15)
        self.two, two_class = classes_of(needs(7), 1.15)
        sizes, three_class = classes_of([three + four for three, four in zip(needs(8), needs(9))], 1.0)
        self.three, self.four = [size[:3] for size in sizes], [size[3:] for size in sizes]
        self.room_one, self.room_two = rooms(self.one), rooms(self.two)
        self.room_three, self.room_four = rooms(self.three), rooms(self.four)

        def branches(which_class, direction):
            pairs = [(n, case[direction]) for n, case in zip(which_class, cases)]
            found = sorted(set(pairs))
            return found, [found.index(pair) for pair in pairs]

        self.one_branches, one_at = branches(one_class, 0)
        self.two_branches, two_at = branches(two_class, 1)
        self.three_branches, three_at = branches(three_class, 2)
        self.flags = dict(
            three_class=three_class,
            one_at=one_at, two_at=two_at, three_at=three_at,
            a=[offsets(*pair)[0] for pair in PAIRS], big_a=[offsets(*pair)[1] for pair in PAIRS],
        )

        found = {}
        for n, (come, ahead, back, fine, coarse, quarters, one, two, three, four) in enumerate(cases):

            def send(exchanged, room):
                return [n for (numbers, _), size in zip(exchanged, room) for n in numbers + [-1] * (size - len(numbers))]

            def source(held, *exchanges):
                places = list(held)
                for exchanged, room in exchanges:
                    for (_, got), size in zip(exchanged, room):
                        places += got + [None] * (size - len(got))
                return {p: n for n, p in enumerate(places) if p is not None}

            first, second = source(block, (one, self.room_one)), source(fine, (two, self.room_two))
            third = source(coarse, (three, self.room_three))
            last = source(fine, (two, self.room_two), (four, self.room_four))
            out = [(l, r, c) for r in range(crows) for c in range(ccols) for l in range(2)]
            rows_of = dict(
                send_one=send(one, self.room_one),
                take_one=[first[p] for p in fine],
                send_two=send(two, self.room_two),
                take_two=[second[p] for p in quarters],
                send_three=send(three, self.room_three),
                send_four=send(four, self.room_four),
                fine_out=[last[p] for p in block],
                coarse_out=[third[p] for p in out],
            )
            for name, row in rows_of.items():
                found.setdefault(name, []).append(row)
        parts, self.at, top = [], {}, 0
        for name, lists in found.items():
            length = -(-max(len(row) for row in lists) // 128)
            part = np.full((len(PAIRS), length * 128), -1, np.float32)
            for n, row in enumerate(lists):
                part[n, : len(row)] = row
            parts.append(part.reshape(len(PAIRS), length, 128))
            self.at[name] = (top, length)
            top += length
        parts.append(np.zeros((len(PAIRS), -top % 8, 128), np.float32))
        self.table = np.concatenate(parts, axis=1)


def case_of(shifts_ref):
    t0, t1 = shifts_ref[0], shifts_ref[1]
    return jnp.where(t0 == WH - 1, t1 - 1, t0 + WH - 2)


def lookup(values, case):
    out = jnp.int32(values[0])
    for n, value in enumerate(values[1:], 1):
        out = jnp.where(case == n, value, out)
    return out


def columns_of(rows, count):
    parts = [jnp.broadcast_to(rows[j : j + 1], (128, 128)).T for j in range(-(-count // 128))]
    return stack_rows(parts)[:count]


def select_rows(index, source):
    lane = lax.broadcasted_iota(I32, (1, 128), 1).astype(F32)
    size = source.shape[0]
    pick = [jnp.where(index == lane + float(at), 1.0, 0.0).astype(BF16) for at in range(0, size, 128)]
    pick = jnp.concatenate(pick, axis=1)[:, :size]
    return jnp.dot(pick, source, preferred_element_type=F32)


def stack_rows(parts):
    return parts[0] if len(parts) == 1 else jnp.concatenate(parts, axis=0)


def layer_norm(values):
    center = jnp.mean(values, axis=-1, keepdims=True)
    values = values - center
    spread = jnp.mean(values * values, axis=-1, keepdims=True)
    return values * lax.rsqrt(spread + EPS)


def attend_windows(qkv_of, id_of, windows, inner, finish):
    lane = lax.broadcasted_iota(I32, (1, 128), 1)
    forbid = jnp.where(lane < 8, BIG, 0.0).astype(BF16)
    groups = inner // 128
    units = [(w, g) for w in range(windows) for g in range(groups)]
    scores, weights, outs = {}, {}, {}

    def score(w, g):
        key_id = id_of(w)
        not_id = (key_id - 1).astype(BF16) * forbid
        q = qkv_of(w, g * 128)
        keys = jnp.concatenate([qkv_of(w, inner + g * 128), key_id], axis=1)
        queries = []
        for h in range(4):
            mine = jnp.where((lane >= h * HD) & (lane < (h + 1) * HD), 1.0, 0.0).astype(BF16)
            queries.append(jnp.concatenate([q * mine, not_id], axis=1))
        scores[w, g] = lax.dot_general(stack_rows(queries), keys, NT, preferred_element_type=F32)

    def soften(w, g):
        s = scores.pop((w, g))
        weights[w, g] = jnp.exp2((s - jnp.max(s, axis=1, keepdims=True)) * SCALE).astype(BF16)

    def gather(w, g):
        v = qkv_of(w, 2 * inner + g * 128)
        values = jnp.concatenate([v, jnp.ones_like(v)], axis=1)
        out = jnp.dot(weights.pop((w, g)), values, preferred_element_type=F32)
        out = out[:, :128] * (1.0 / out[:, 128:])
        picked = out[:TOK]
        for h in range(1, 4):
            picked = jnp.where(lane < h * HD, picked, out[h * TOK : (h + 1) * TOK])
        outs[w, g] = picked.astype(BF16)
        if g == groups - 1:
            finish(w, jnp.concatenate([outs.pop((w, k)) for k in range(groups)], axis=1))

    for n in range(len(units) + 2):
        if n < len(units):
            score(*units[n])
        if 0 <= n - 1 < len(units):
            soften(*units[n - 1])
        if 0 <= n - 2 < len(units):
            gather(*units[n - 2])


ANY = pl.BlockSpec(memory_space=pl.ANY)
HBM = pl.BlockSpec(memory_space=pltpu.HBM)
VMEM = pl.BlockSpec(memory_space=pltpu.VMEM)
SMEM = pl.BlockSpec(memory_space=pltpu.SMEM)


def call(body, outs, args, in_specs, scratch, copies, flops, moved_bytes, vmem=8):
    args = [
        pltpu.with_memory_space_constraint(arg, spec.memory_space) for arg, spec in zip(args, in_specs, strict=True)
    ]
    spaces = [getattr(out, "memory_space", pltpu.SMEM if out.dtype == I32 else pltpu.VMEM) for out in outs]
    out_specs = [pl.BlockSpec(memory_space=space) for space in spaces]
    return pl.pallas_call(
        body,
        out_shape=outs,
        in_specs=in_specs,
        out_specs=out_specs,
        scratch_shapes=list(scratch) + [pltpu.SemaphoreType.DMA((copies,))],
        compiler_params=pltpu.CompilerParams(vmem_limit_bytes=vmem << 20),
        cost_estimate=pl.CostEstimate(flops=flops, bytes_accessed=moved_bytes, transcendentals=0),
    )(*args)


def shapes(sizes, width, space=pltpu.VMEM):
    return [space((n, width), BF16) for n in sizes]


class Copies:
    def __init__(self, sems):
        self.sems, self.used = sems, 0

    def __call__(self, src, dst):
        copy = pltpu.make_async_copy(src, dst, self.sems.at[self.used])
        self.used += 1
        copy.start()
        return copy


def lay(pieces, room):
    width = pieces[0].shape[1]

    def body(*refs):
        out_ref = refs[len(pieces)]
        at = 0
        for ref, space in zip(refs, room):
            rows = ref.shape[0]
            out_ref[at : at + rows, :] = ref[...]
            if rows < space:
                out_ref[at + rows : at + space, :] = jnp.zeros((space - rows, width), BF16)
            at += space

    return call(body, shapes([sum(room)], width), pieces, [VMEM] * 3, [], 1, 0, 1 << 18)[0]


def flat(ref):
    layers, rows, cols, width = ref.shape
    return ref[...].astype(F32).reshape(layers * rows * cols, width).astype(BF16)


def put_pieces(value, refs):
    at = 0
    for ref in refs:
        ref[...] = value[at : at + ref.shape[0]].astype(BF16)
        at += ref.shape[0]


def rows_of(plan, table_ref, name, *lead):
    top, length = plan.at[name]
    return table_ref[(*lead, slice(top, top + length), slice(None))]


def exchange(pieces, sizes, sign):
    lat, lon = lax.axis_size("lat"), lax.axis_size("lon")
    row, col, both = [piece[:size] for piece, size in zip(pieces, sizes)]
    pairs = [((i + sign) % lat * lon + (j + sign) % lon, i * lon + j) for i in range(lat) for j in range(lon)]
    col = lax.ppermute(col, "lon", [((j + sign) % lon, j) for j in range(lon)])
    both = lax.ppermute(both, ("lat", "lon"), pairs)
    row = lax.ppermute(row, "lat", [((i + sign) % lat, i) for i in range(lat)])
    return [row, col, both]


def choose(index, branches, *args):
    flat_args, tree = jax.tree.flatten(args)
    out_trees = []

    def closed(branch):
        def run(*leaves):
            out, out_tree = jax.tree.flatten(branch(*jax.tree.unflatten(tree, leaves)))
            out_trees.append(out_tree)
            return out

        return jax.make_jaxpr(run)(*flat_args)

    out = lax.cond_p.bind(index, *flat_args, branches=tuple(closed(branch) for branch in branches))
    return jax.tree.unflatten(out_trees[0], out)


FLAGS = ("three_class", "a", "big_a")


def first_pieces(shifts, tokens, plan):
    width = tokens.shape[-1]
    count = tokens.size // width
    kinds = 3

    def body(shifts_hbm, tokens_hbm, table_hbm, *refs):
        outs, refs = refs[:kinds], refs[kinds:]
        rows_ref, flags_ref, *at_refs, shifts_ref, tokens_ref, table_ref, source_ref, sems = refs
        start = Copies(sems)
        shift = start(shifts_hbm, shifts_ref)
        held = start(tokens_hbm, tokens_ref)
        table = start(table_hbm, table_ref)
        shift.wait()
        case = case_of(shifts_ref)
        for ref, name in zip(at_refs, ("one_at", "two_at", "three_at")):
            ref[0] = lookup(plan.flags[name], case)
        for n, name in enumerate(FLAGS):
            flags_ref[n] = lookup(plan.flags[name], case)
        held.wait()
        source_ref[...] = flat(tokens_ref)
        table.wait()
        rows_ref[...] = table_ref[case]
        index = columns_of(rows_of(plan, table_ref, "send_one", case), sum(plan.room_one))
        put_pieces(select_rows(index, source_ref[...]), outs)

    outs = shapes(plan.room_one, width)
    outs += [pltpu.VMEM(plan.table.shape[1:], F32), pltpu.SMEM((8,), I32)]
    outs += [pltpu.SMEM((1,), I32)] * 3
    scratch = [pltpu.SMEM((2,), I32), pltpu.VMEM(tokens.shape, BF16), pltpu.VMEM(plan.table.shape, F32)]
    scratch += [pltpu.VMEM((count, width), BF16)]
    got = call(body, outs, [shifts, tokens, plan.table], [HBM] * 3, scratch, 3, 1 << 28, 1 << 20)
    sent, (rows, flags, one, two, three) = got[:kinds], got[kinds:]
    return sent, rows, flags, one[0], two[0], three[0]


def before_fine(flags, regions, tokens, table, weights, plan):
    _, lat, lon = regions.shape
    _, rows, cols, width = tokens.shape
    flat_regions = regions.reshape(2 * lat, lon)
    fine, coarse = windowed(rows, cols), natural(rows // 2, cols // 2)

    def lanes(places, scale, is_fine):
        places = np.asarray([(l, scale * r, scale * c, is_fine) for l, r, c in places], np.float32)
        return np.pad(places, ((0, -len(places) % 128), (0, 0))).T.reshape(4, -1, 128)

    places = np.concatenate([lanes(fine, 1, 1), lanes(coarse, 2, 0)], axis=1)
    lines = places.shape[1]
    count = 128 * lines

    def body(flags_ref, rows_ref, regions_hbm, places_hbm, tokens_hbm, *refs):
        weights_hbm, refs = refs[: len(weights)], refs[len(weights) :]
        id_ref, x_ref, *refs = refs
        weight_refs, (regions_ref, places_ref, tokens_ref, sems) = refs[: len(weights)], refs[len(weights) :]
        start = Copies(sems)
        waits = [start(regions_hbm, regions_ref), start(places_hbm, places_ref)]
        held = start(tokens_hbm, tokens_ref)
        later = [start(src, dst) for src, dst in zip(weights_hbm, weight_refs)]
        for copy in waits:
            copy.wait()
        a = flags_ref[1].astype(F32)
        big_a = 2.0 * flags_ref[2].astype(F32)
        is_fine = places_ref[3]
        d = is_fine * a + (1.0 - is_fine) * big_a
        row = places_ref[1] + d + (lax.axis_index("lat") * rows).astype(F32)
        col = places_ref[2] + 2.0 * d + (lax.axis_index("lon") * cols).astype(F32)
        wrapped = jnp.where((row < 0) | (row >= lat), 4.0, 0.0)
        row = jnp.where(row < 0, row + lat, jnp.where(row >= lat, row - lat, row))
        col = jnp.where(col < 0, col + lon, jnp.where(col >= lon, col - lon, col))
        row = columns_of(row + places_ref[0] * lat, count)
        col = columns_of(col, count)
        wrapped = columns_of(wrapped, count)
        picked = select_rows(row, regions_ref[...].astype(F32).astype(BF16))
        ids = jnp.zeros((count, 128), F32)
        for at in range(0, lon, 128):
            size = min(128, lon - at)
            lane = lax.broadcasted_iota(I32, (1, size), 1).astype(F32) + float(at)
            here = jnp.where(lane == col[:, :size], picked[:, at : at + size], 0.0)
            ids = ids + jnp.sum(here, axis=1, keepdims=True)
        ids = ids + wrapped
        for n in range(lines):
            id_ref[n : n + 1, :] = ids[n * 128 : (n + 1) * 128].T[:1]
        held.wait()
        take = columns_of(rows_of(plan, rows_ref, "take_one"), len(fine))
        x_ref[...] = select_rows(take, flat(tokens_ref)).astype(BF16)
        for copy in later:
            copy.wait()

    outs = [pltpu.VMEM((lines, 128), F32)] + shapes([len(fine)], width)
    outs += [pltpu.VMEM(w.shape, BF16) for w in weights]
    scratch = [pltpu.VMEM(flat_regions.shape, I32), pltpu.VMEM(places.shape, F32), pltpu.VMEM(tokens.shape, BF16)]
    args = [flags, table, flat_regions, places, tokens, *weights]
    in_specs = [SMEM, VMEM] + [HBM] * (3 + len(weights))
    ids, x, *weights = call(body, outs, args, in_specs, scratch, 3 + len(weights), 1 << 28, 4 << 20)
    return ids, x, weights


def id_columns(lines, count):
    lane = lax.broadcasted_iota(I32, (1, 128), 1).astype(F32)
    return jnp.where(columns_of(lines, count) == lane, 1.0, 0.0).astype(BF16)


def before_coarse(fine, table, weight, plan):
    own, width = fine.shape
    half = 3 * weight.shape[0] // 8

    def body(rows_ref, fine_hbm, weight_hbm, x_ref, part_hbm, weight_ref, fine_ref, part_ref, sems):
        start = Copies(sems)
        held = start(fine_hbm, fine_ref)
        later = start(weight_hbm.at[pl.ds(0, half)], weight_ref)
        take = columns_of(rows_of(plan, rows_ref, "fine_out"), own)
        held.wait()
        part_ref[...] = select_rows(take, fine_ref[...]).astype(BF16)
        leave = start(part_ref, part_hbm)
        take = columns_of(rows_of(plan, rows_ref, "take_two"), own)
        x_ref[...] = select_rows(take, fine_ref[...]).astype(BF16)
        leave.wait()
        later.wait()

    outs = shapes([own], width) + shapes([own], width, pltpu.HBM) + shapes([half], weight.shape[1])
    scratch = [pltpu.VMEM(fine.shape, BF16)] * 2
    return call(body, outs, [table, fine, weight], [VMEM, HBM, HBM], scratch, 3, 1 << 28, 4 << 20)


def fine_level(x_own, source, ids, w_qkv, w_proj, rows, plan):
    count, width = x_own.shape
    inner = w_proj.shape[0]

    def body(own_ref, source_ref, ids_ref, qkv_w_ref, proj_w_ref, rows_ref, out_hbm, *refs):
        *piece_outs, x_ref, qkv_ref, out_ref, id_ref, sems = refs
        start = Copies(sems)
        id_ref[...] = id_columns(ids_ref[: -(-count // 128), :], count)
        leave = []
        take = columns_of(rows_of(plan, rows_ref, "take_one"), count) - float(count)
        x = own_ref[...].astype(F32) + select_rows(take, source_ref[...])
        x_ref[...] = x
        normed = layer_norm(x).astype(BF16)
        qkv_ref[...] = jnp.dot(normed, qkv_w_ref[...], preferred_element_type=F32).astype(BF16)

        def finish(w, out):
            at = slice(w * TOK, (w + 1) * TOK)
            out = jnp.dot(out, proj_w_ref[...], preferred_element_type=F32)
            out_ref[at, :] = (x_ref[at, :] + out).astype(BF16)
            leave.append(start(out_ref.at[pl.ds(w * TOK, TOK)], out_hbm.at[pl.ds(w * TOK, TOK)]))

        attend_windows(
            lambda w, at: qkv_ref[w * TOK : (w + 1) * TOK, at : at + 128],
            lambda w: id_ref[w * TOK : (w + 1) * TOK, :],
            count // TOK,
            inner,
            finish,
        )
        index = columns_of(rows_of(plan, rows_ref, "send_two"), sum(plan.room_two))
        put_pieces(select_rows(index, out_ref[...]), piece_outs)
        for copy in leave:
            copy.wait()

    outs = shapes([count], width, pltpu.HBM) + shapes(plan.room_two, width)
    scratch = [
        pltpu.VMEM((count, width), F32),
        pltpu.VMEM((count, 3 * inner), BF16),
        pltpu.VMEM((count, width), BF16),
        pltpu.VMEM((count, 128), BF16),
    ]
    args = [x_own, source, ids, w_qkv, w_proj, rows]
    out, *sent = call(body, outs, args, [VMEM] * len(args), scratch, count // TOK, 3 << 30, 6 << 20, 14)
    return out, sent


def coarse_level(flags, fine, x_own, source, ids, merge_first, w_merge, w_qkv, w_proj, rows, plan):
    depth, width = w_merge.shape
    own, half = fine.shape
    count = own // 4
    inner = w_proj.shape[0]

    def body(
        flags_ref, fine_hbm, merge_hbm, qkv_w_hbm, proj_w_hbm, own_ref, source_ref, ids_ref, first_ref, rows_ref, *refs
    ):
        out_ref, *piece_outs = refs[:4]
        qkv_ref, fine_ref, id_ref, merge_ref, qkv_w_ref, proj_w_ref, sems = refs[4:]
        start = Copies(sems)
        with_fine = [n for n, sizes in enumerate(plan.four) if sum(sizes)]
        needs_fine = functools.reduce(jnp.logical_or, [flags_ref[0] == n for n in with_fine])

        def bring(src, dst):
            cuts = [(at, min(half, src.shape[0] - at)) for at in range(0, src.shape[0], half)]
            return [(at, size, start(src.at[pl.ds(at, size)], dst.at[pl.ds(at, size)])) for at, size in cuts]

        def product(x, ref, copies):
            parts = []
            for at, size, copy in copies:
                copy.wait()
                parts.append(jnp.dot(x[:, at : at + size], ref[at : at + size, :], preferred_element_type=F32))
            return functools.reduce(jnp.add, parts)

        here = first_ref.shape[0]
        merge_w = bring(merge_hbm.at[pl.ds(here, depth - here)], merge_ref)
        qkv_w = bring(qkv_w_hbm, qkv_w_ref)
        proj_w = start(proj_w_hbm, proj_w_ref)
        fine_copy = (fine_hbm, fine_ref, sems.at[start.used])

        @pl.when(needs_fine)
        def _():
            pltpu.make_async_copy(*fine_copy).start()

        id_ref[...] = id_columns(ids_ref[-(-own // 128) :, :], count)
        take = columns_of(rows_of(plan, rows_ref, "take_two"), 4 * count) - float(own)
        x = own_ref[...].astype(F32) + select_rows(take, source_ref[...])
        x = jnp.concatenate([x[n * count : (n + 1) * count] for n in range(4)], axis=1)
        stacked = layer_norm(x).astype(BF16)
        merged = jnp.dot(stacked[:, :here], first_ref[...], preferred_element_type=F32)
        merged = (merged + product(stacked[:, here:], merge_ref, merge_w)).astype(BF16).astype(F32)
        normed = layer_norm(merged).astype(BF16)
        qkv_ref[...] = product(normed, qkv_w_ref, qkv_w).astype(BF16)
        proj_w.wait()

        def finish(w, out):
            out = jnp.dot(out, proj_w_ref[...], preferred_element_type=F32)
            out_ref[...] = (merged + out).astype(BF16)

        attend_windows(lambda w, at: qkv_ref[:, at : at + 128], lambda w: id_ref[...], 1, inner, finish)
        sent = select_rows(columns_of(rows_of(plan, rows_ref, "send_three"), sum(plan.room_three)), out_ref[...])
        sent = sent.astype(BF16)
        for n, sizes in enumerate(plan.three):

            @pl.when(flags_ref[0] == n)
            def _():
                at = 0
                for ref, size, space in zip(piece_outs, sizes, plan.room_three):
                    ref[:size, :] = sent[at : at + size, :half]
                    ref[size : 2 * size, :] = sent[at : at + size, half:]
                    at += space

        @pl.when(needs_fine)
        def _():
            pltpu.make_async_copy(*fine_copy).wait()
            index = columns_of(rows_of(plan, rows_ref, "send_four"), sum(plan.room_four))
            sent = select_rows(index, fine_ref[...]).astype(BF16)
            for n in with_fine:

                @pl.when(flags_ref[0] == n)
                def _():
                    at = 0
                    for ref, size, more, space in zip(piece_outs, plan.three[n], plan.four[n], plan.room_four):
                        ref[2 * size : 2 * size + more, :] = sent[at : at + more]
                        at += space

    most = [max(2 * three[k] + four[k] for three, four in zip(plan.three, plan.four)) for k in range(3)]
    outs = shapes([count], width) + shapes(most, half)
    scratch = [pltpu.VMEM((count, 3 * inner), BF16)]
    shapes_in = [fine.shape, (count, 128), (depth - merge_first.shape[0], width), w_qkv.shape, w_proj.shape]
    scratch += [pltpu.VMEM(shape, BF16) for shape in shapes_in]
    args = [flags, fine, w_merge, w_qkv, w_proj, x_own, source, ids, merge_first, rows]
    in_specs = [SMEM] + [HBM] * 4 + [VMEM] * (len(args) - 5)
    copies = depth // half + width // half + 3
    out, *sent = call(body, outs, args, in_specs, scratch, copies, 3 << 30, 12 << 20, 24)
    return out, sent


def fine_output(part, source, rows, plan, block_rows, block_cols, partial):
    own, width = part.shape

    def body(part_hbm, source_ref, rows_ref, out_ref, part_ref, stage_ref, sems):
        start = Copies(sems)
        cuts = [pl.ds(at, TOK) for at in range(0, own, TOK)]
        held = [start(part_hbm.at[cut], part_ref.at[cut]) for cut in cuts]
        take = columns_of(rows_of(plan, rows_ref, "fine_out"), own) - float(own)
        leave = []
        for n, (cut, copy) in enumerate(zip(cuts, held)):
            got = select_rows(take[n * TOK : (n + 1) * TOK], source_ref[...])
            copy.wait()
            out = part_ref[cut, :].astype(F32) + got
            if partial:
                out_ref[cut, :] = out.astype(BF16)
            else:
                lines = TOK // block_cols
                layer, line = divmod(n * lines, block_rows)
                there = (layer, pl.ds(line, lines))
                stage_ref[there] = out.reshape(lines, block_cols, width).astype(BF16)
                leave.append(start(stage_ref.at[there], out_ref.at[there]))
        for copy in leave:
            copy.wait()

    shape = (2, block_rows, block_cols, width)
    outs = shapes([own], width) if partial else [pltpu.HBM(shape, BF16)]
    scratch = [pltpu.VMEM(part.shape, BF16), pltpu.VMEM(shape, BF16)]
    return call(body, outs, [part, source, rows], [HBM, VMEM, VMEM], scratch, 2 * own // TOK, 1 << 30, 4 << 20)[0]


def coarse_output(coarse, got, rows, which, plan, block_rows, block_cols, part=None):
    own, width = coarse.shape
    half = width // 2
    sizes, more = plan.three[which], plan.four[which]
    parts = [] if part is None else [part]

    def padded(parts, sizes, room):
        out = []
        for value, size, space in zip(parts, sizes, room):
            out.append(value)
            if size < space:
                out.append(jnp.zeros((space - size, value.shape[1]), F32))
        return out

    def body(coarse_ref, *refs):
        got_refs, refs = refs[:3], refs[3:]
        part_refs, (rows_ref, out_ref, *fine_outs, _) = refs[: len(parts)], refs[len(parts) :]
        got = [ref[...].astype(F32) for ref in got_refs]
        back = [jnp.concatenate([x[:size], x[size : 2 * size]], axis=1) for x, size in zip(got, sizes)]
        source = stack_rows([coarse_ref[...].astype(F32)] + padded(back, sizes, plan.room_three))
        out = select_rows(columns_of(rows_of(plan, rows_ref, "coarse_out"), own), source.astype(BF16)).astype(BF16)
        for n in range(own // 2):
            out_ref[n // block_cols, n % block_cols] = out[2 * n : 2 * n + 2]
        for part_ref, fine_ref in zip(part_refs, fine_outs):
            fine = stack_rows(padded([x[2 * size :] for x, size in zip(got, sizes)], more, plan.room_four))
            base = part_ref.shape[0] + sum(plan.room_two)
            take = columns_of(rows_of(plan, rows_ref, "fine_out"), part_ref.shape[0]) - float(base)
            out = part_ref[...].astype(F32) + select_rows(take, fine.astype(BF16))
            fine_ref[...] = out.reshape(fine_ref.shape).astype(BF16)

    outs = [jax.ShapeDtypeStruct((block_rows, block_cols, 2, width), BF16)]
    outs += [jax.ShapeDtypeStruct((2, 2 * block_rows, 2 * block_cols, half), BF16) for _ in parts]
    args = [coarse, *got, *parts, rows]
    out, *fine = call(body, outs, args, [VMEM] * len(args), [], 1, 1 << 28, 1 << 20)
    return out.transpose(2, 0, 1, 3), *fine


def on_device(tokens, regions, shifts, fine_qkv, fine_proj, merge_weight, coarse_qkv, coarse_proj):
    _, rows, cols, _ = tokens.shape
    plan = Plan(rows, cols)

    def first(which, sign, sent, *args):
        got = exchange(sent, plan.one[which], sign)
        return lay(got, plan.room_one), before_fine(*args, plan)

    def second(which, sign, sent, *args):
        got = exchange(sent, plan.two[which], sign)
        return lay(got, plan.room_two), before_coarse(*args, plan)

    def third(which, sign, sent, part, source, coarse, table):
        sizes = [2 * n + m for n, m in zip(plan.three[which], plan.four[which])]
        got = exchange(sent, sizes, sign)
        partial = sum(plan.four[which]) > 0
        fine_out = fine_output(part, source, table, plan, rows, cols, partial)
        place = (table, which, plan, rows // 2, cols // 2)
        if partial:
            coarse_out, fine_out = coarse_output(coarse, got, *place, part=fine_out)
        else:
            (coarse_out,) = coarse_output(coarse, got, *place)
        return fine_out, coarse_out

    def branches(stage, pairs):
        return [functools.partial(stage, which, sign) for which, sign in pairs]

    sent, table, flags, one, two, three = first_pieces(shifts, tokens, plan)
    got, (ids, x, weights) = choose(
        one, branches(first, plan.one_branches), sent, flags, regions, tokens, table, [fine_qkv, fine_proj]
    )
    fine, sent = fine_level(x, got, ids, *weights, table, plan)
    got, (x, part, merge_first) = choose(two, branches(second, plan.two_branches), sent, fine, table, merge_weight)
    coarse, sent = coarse_level(
        flags, fine, x, got, ids, merge_first, merge_weight, coarse_qkv, coarse_proj, table, plan
    )
    return choose(three, branches(third, plan.three_branches), sent, part, got, coarse, table)


def solution(mesh):
    return jax.shard_map(
        on_device,
        mesh=mesh,
        in_specs=(P(None, "lat", "lon", None), P(), P(), P(), P(), P(), P(), P()),
        out_specs=(P(None, "lat", "lon", None), P(None, "lat", "lon", None)),
        check_vma=False,
    )
```

profile of v0, /device:TPU:0, one launch (start us, length us, event | category | flops | bytes accessed | tf_op | source)
XLA Modules:
  0.0 39.0 jit_solution(10508972676506011609)
XLA Ops:
  0.6 1.6 %shard_map.116 = (bf16[112,512]{1,0:T(8,128)(2,1)S(1)}, bf16[112,512]{1,0:T(8,128)(2,1)S(1)}, bf16[48,512]{1,0:T(8,128)(2,1)S(1)}, f32[32,128]{1,0:T(8,128)S(1)}...) custom-call(s32[2]{0:T(128)} %shifts_hbm.1, bf16[2,12,24,512]{3,2,1,0:T(8,128)(2,1)} %tokens_hbm.1, ...), custom_call_target="tpu_custom_call" | custom-call | flops 268435456 | bytes 1048576 | tf_op jit(solution)/shard_map/pallas_call | solution.py:273
  2.2 10.1 %conditional.3 = (bf16[272,512]{1,0:T(8,128)(2,1)S(1)}, f32[7,128]{1,0:T(8,128)S(1)}, bf16[576,512]{1,0:T(8,128)(2,1)S(1)}, bf16[512,1536]{1,0:T(8,128)(2,1)S(1)}, bf16[512,512]{1,0:T(8,128)(2,1)S(1)}) conditional(s32[]{:T(128)S(4)} %bitcast.13, (bf16[112,512]{1,0:T(8,128)(2,1)S(1)}, bf16[112,512]{1,0:T(8,128)(2,1)S(1)}, ...), branch_computations={%region_0.0_spmd, %region_1.0_spmd, %region_2.0_spmd, %region_3.0_... | conditional | flops 268435456 | bytes 5619872 | solution.py:354
  2.2 3.1 %collective-permute-start.1 = (bf16[48,512]{1,0:T(8,128)(2,1)S(1)}, bf16[48,512]{1,0:T(8,128)(2,1)S(1)}, u32[]{:S(2)}, u32[]{:S(2)}) collective-permute-start(bf16[48,512]{1,0:T(8,128)(2,1)S(1)} %slice.91), channel_id=1, source_target_pairs={{3,0},{0,1},{1,2},{2,3},{7,4},{4,5},{5,6},{6,7},{11,8},{8,9},{9,10... | collective-permute-start | bytes 147464 | tf_op jit(solution)/shard_map/cond/branch_0_fun/ppermute | solution.py:336
  5.3 0.0 collective-permute-start
  5.3 2.8 %collective-permute-start.2 = (bf16[8,512]{1,0:T(8,128)(2,1)S(1)}, bf16[8,512]{1,0:T(8,128)(2,1)S(1)}, u32[]{:S(2)}, u32[]{:S(2)}) collective-permute-start(bf16[8,512]{1,0:T(8,128)(2,1)S(1)} %slice.92), channel_id=1, source_target_pairs={{31,0},{28,1},{29,2},{30,3},{3,4},{0,5},{1,6},{2,7},{7,8},{4,9},{5... | collective-permute-start | bytes 24584 | tf_op jit(solution)/shard_map/cond/branch_0_fun/ppermute | solution.py:337
  8.1 2.4 %branch_0_fun.7 = (f32[7,128]{1,0:T(8,128)S(1)}, bf16[576,512]{1,0:T(8,128)(2,1)S(1)}, bf16[512,1536]{1,0:T(8,128)(2,1)S(1)}, bf16[512,512]{1,0:T(8,128)(2,1)S(1)}) custom-call(s32[8]{0:T(128)S(4)} %get-tuple-element.261.flags_ref, f32[32,128]{1,0:T(8,128)S(1)} %get-tuple-element.262.rows_ref, s32[192,96]{1,0:T(8,128)} %bitcast.14, ...), custom_call_target="tpu_custom_call" | custom-call | flops 268435456 | bytes 4194304 | tf_op jit(solution)/shard_map/cond/branch_0_fun/pallas_call | solution.py:273
  10.5 1.6 %collective-permute-done.2.refs_2_ = bf16[8,512]{1,0:T(8,128)(2,1)S(1)} collective-permute-done((bf16[8,512]{1,0:T(8,128)(2,1)S(1)}, bf16[8,512]{1,0:T(8,128)(2,1)S(1)}, u32[]{:S(2)}, u32[]{:S(2)}) %collective-permute-start.2) | collective-permute-done | bytes 8224 | tf_op jit(solution)/shard_map/cond/branch_0_fun/ppermute | solution.py:337
  12.1 0.0 collective-permute-done.1.refs_1_
  12.1 0.0 collective-permute-done.refs_0_
  12.3 5.9 %shard_map.117 = (bf16[576,512]{1,0:T(8,128)(2,1)}, bf16[160,512]{1,0:T(8,128)(2,1)S(1)}, bf16[160,512]{1,0:T(8,128)(2,1)S(1)}, bf16[112,512]{1,0:T(8,128)(2,1)S(1)}) custom-call(bf16[576,512]{1,0:T(8,128)(2,1)S(1)} %get-tuple-element.469.own_ref, bf16[272,512]{1,0:T(8,128)(2,1)S(1)} %get-tuple-element.470.source_ref, ...), custom_call_target="tpu_custom_call" | custom-call | flops 3221225472 | bytes 6291456 | tf_op jit(solution)/shard_map/pallas_call | solution.py:273
  18.2 7.6 %conditional.4 = (bf16[432,512]{1,0:T(8,128)(2,1)S(1)}, bf16[576,512]{1,0:T(8,128)(2,1)S(1)}, bf16[576,512]{1,0:T(8,128)(2,1)}, bf16[768,1024]{1,0:T(8,128)(2,1)S(1)}) conditional(s32[]{:T(128)S(4)} %bitcast.12, (bf16[160,512]{1,0:T(8,128)(2,1)S(1)}, bf16[160,512]{1,0:T(8,128)(2,1)S(1)}, ...), branch_computations={%region_5.0_spmd, %region_6.0_spmd, %region_7.0_spmd, %region_8.0_... | conditional | flops 268435456 | bytes 6619288 | solution.py:354
  18.3 0.1 collective-permute-start.16
  18.4 0.1 collective-permute-start.15
  18.5 1.5 %collective-permute-start.17 = (bf16[8,512]{1,0:T(8,128)(2,1)S(1)}, bf16[8,512]{1,0:T(8,128)(2,1)S(1)}, u32[]{:S(2)}, u32[]{:S(2)}) collective-permute-start(bf16[8,512]{1,0:T(8,128)(2,1)S(1)} %slice.105), channel_id=1, source_target_pairs={{31,0},{28,1},{29,2},{30,3},{3,4},{0,5},{1,6},{2,7},{7,8},{4,9},{5... | collective-permute-start | bytes 24584 | tf_op jit(solution)/shard_map/cond/branch_0_fun/ppermute | solution.py:337
  20.0 2.6 %branch_0_fun.9 = (bf16[576,512]{1,0:T(8,128)(2,1)S(1)}, bf16[576,512]{1,0:T(8,128)(2,1)}, bf16[768,1024]{1,0:T(8,128)(2,1)S(1)}) custom-call(f32[32,128]{1,0:T(8,128)S(1)} %get-tuple-element.326.rows_ref, bf16[576,512]{1,0:T(8,128)(2,1)} %get-tuple-element.327.fine_hbm, bf16[2048,1024]{1,0:T(8,128)(2,1)} %get-tuple-element.328.weight_hbm), custom_call_target="tpu_custom_call" | custom-call | flops 268435456 | bytes 4194304 | tf_op jit(solution)/shard_map/cond/branch_0_fun/pallas_call | solution.py:273
  22.6 3.0 %collective-permute-done.17.refs_2_ = bf16[8,512]{1,0:T(8,128)(2,1)S(1)} collective-permute-done((bf16[8,512]{1,0:T(8,128)(2,1)S(1)}, bf16[8,512]{1,0:T(8,128)(2,1)S(1)}, u32[]{:S(2)}, u32[]{:S(2)}) %collective-permute-start.17) | collective-permute-done | bytes 8224 | tf_op jit(solution)/shard_map/cond/branch_0_fun/ppermute | solution.py:337
  25.6 0.0 collective-permute-done.16.refs_1_
  25.6 0.0 collective-permute-done.15.refs_0_
  25.9 5.1 %shard_map.118 = (bf16[144,1024]{1,0:T(8,128)(2,1)S(1)}, bf16[128,512]{1,0:T(8,128)(2,1)S(1)}, bf16[128,512]{1,0:T(8,128)(2,1)S(1)}, bf16[88,512]{1,0:T(8,128)(2,1)S(1)}) custom-call(s32[8]{0:T(128)S(4)} %get-tuple-element.467.flags_ref, bf16[576,512]{1,0:T(8,128)(2,1)} %get-tuple-element.477.fine_hbm, bf16[2048,1024]{1,0:T(8,128)(2,1)} %merge_hbm.1, ...), custom_call_target="tpu_custom_call" | custom-call | flops 3221225472 | bytes 12582912 | tf_op jit(solution)/shard_map/pallas_call | solution.py:273
  31.0 7.9 %conditional.5 = (bf16[2,12,24,512]{3,2,1,0:T(8,128)(2,1)}, bf16[2,6,12,1024]{3,0,2,1:T(2,128)(2,1)}) conditional(s32[]{:T(128)S(4)} %bitcast.11, (bf16[576,512]{1,0:T(8,128)(2,1)}, bf16[432,512]{1,0:T(8,128)(2,1)S(1)}, f32[32,128]{1,0:T(8,128)S(1)}, bf16[128,512]{1,0:T(8,128)(2,1)S(1)}, ...), branch_computations={%region_12.0_spmd, %region_13.0_spmd, %region_14.0_spmd, %region_1... | conditional | flops 1342177280 | bytes 6865032 | solution.py:354
  31.0 1.8 %collective-permute-start.47 = (bf16[24,512]{1,0:T(8,128)(2,1)S(1)}, bf16[24,512]{1,0:T(8,128)(2,1)S(1)}, u32[]{:S(2)}, u32[]{:S(2)}) collective-permute-start(bf16[24,512]{1,0:T(8,128)(2,1)S(1)} %slice.131), channel_id=1, source_target_pairs={{5,0},{6,1},{7,2},{4,3},{9,4},{10,5},{11,6},{8,7},{13,8},{14,9},{1... | collective-permute-start | bytes 73736 | tf_op jit(solution)/shard_map/cond/branch_3_fun/ppermute | solution.py:337
  32.8 1.1 %collective-permute-start.46 = (bf16[96,512]{1,0:T(8,128)(2,1)S(1)}, bf16[96,512]{1,0:T(8,128)(2,1)S(1)}, u32[]{:S(2)}, u32[]{:S(2)}) collective-permute-start(bf16[96,512]{1,0:T(8,128)(2,1)S(1)} %slice.130), channel_id=1, source_target_pairs={{1,0},{2,1},{3,2},{0,3},{5,4},{6,5},{7,6},{4,7},{9,8},{10,9},{11,1... | collective-permute-start | bytes 294920 | tf_op jit(solution)/shard_map/cond/branch_3_fun/ppermute | solution.py:336
  33.9 0.6 %collective-permute-start.45 = (bf16[96,512]{1,0:T(8,128)(2,1)S(1)}, bf16[96,512]{1,0:T(8,128)(2,1)S(1)}, u32[]{:S(2)}, u32[]{:S(2)}) collective-permute-start(bf16[96,512]{1,0:T(8,128)(2,1)S(1)} %slice.129), channel_id=1, source_target_pairs={{4,0},{8,4},{12,8},{16,12},{20,16},{24,20},{28,24},{0,28},{5,1},{9... | collective-permute-start | bytes 294920 | tf_op jit(solution)/shard_map/cond/branch_3_fun/ppermute | solution.py:338
  34.5 1.9 %branch_3_fun.10.refs_3_ = bf16[576,512]{1,0:T(8,128)(2,1)S(1)} custom-call(bf16[576,512]{1,0:T(8,128)(2,1)} %get-tuple-element.411.part_hbm, bf16[432,512]{1,0:T(8,128)(2,1)S(1)} %get-tuple-element.412.source_ref, f32[32,128]{1,0:T(8,128)S(1)} %get-tuple-element.413.rows_ref.refs_4_), custom_call_target="tpu_custom_call" | custom-call | flops 1073741824 | bytes 4194304 | tf_op jit(solution)/shard_map/cond/branch_3_fun/pallas_call | solution.py:273
  36.3 0.0 collective-permute-done.47.refs_2_
  36.4 1.1 %collective-permute-done.46.refs_1_ = bf16[96,512]{1,0:T(8,128)(2,1)S(1)} collective-permute-done((bf16[96,512]{1,0:T(8,128)(2,1)S(1)}, bf16[96,512]{1,0:T(8,128)(2,1)S(1)}, u32[]{:S(2)}, u32[]{:S(2)}) %collective-permute-start.46) | collective-permute-done | bytes 98336 | tf_op jit(solution)/shard_map/cond/branch_3_fun/ppermute | solution.py:336
  37.5 0.0 collective-permute-done.45.refs_0_
  37.5 1.4 %branch_3_fun.11 = (bf16[6,12,2,1024]{3,2,1,0:T(2,128)(2,1)}, bf16[2,12,24,512]{3,2,1,0:T(8,128)(2,1)}) custom-call(bf16[144,1024]{1,0:T(8,128)(2,1)S(1)} %get-tuple-element.407.coarse_ref, bf16[96,512]{1,0:T(8,128)(2,1)S(1)} %collective-permute-done.45.refs_0_, bf16[96,512]{1,0:T(8,128)(2,1)S(1)} %collective-permute-done.46.refs_1_, ...), custom_call_target="tpu_custom_call" | custom-call | flops 268435456 | bytes 1048576 | tf_op jit(solution)/shard_map/cond/branch_3_fun/pallas_call | solution.py:273
  (11 shorter events, 0.1 us)
Async XLA Ops:
  2.2 9.8 %collective-permute-start.1 = (bf16[48,512]{1,0:T(8,128)(2,1)S(1)}, bf16[48,512]{1,0:T(8,128)(2,1)S(1)}, u32[]{:S(2)}, u32[]{:S(2)}) collective-permute-start(bf16[48,512]{1,0:T(8,128)(2,1)S(1)} %slice.91), channel_id=1, source_target_pairs={{3,0},{0,1},{1,2},{2,3},{7,4},{4,5},{5,6},{6,7},{11,8},{8,9},{9,10... | collective-permute-start | bytes 147464 | tf_op jit(solution)/shard_map/cond/branch_0_fun/ppermute | solution.py:336
  5.3 6.7 %collective-permute-start = (bf16[48,512]{1,0:T(8,128)(2,1)S(1)}, bf16[48,512]{1,0:T(8,128)(2,1)S(1)}, u32[]{:S(2)}, u32[]{:S(2)}) collective-permute-start(bf16[48,512]{1,0:T(8,128)(2,1)S(1)} %slice.90), channel_id=1, source_target_pairs={{28,0},{0,4},{4,8},{8,12},{12,16},{16,20},{20,24},{24,28},{29,1},{... | collective-permute-start | bytes 147464 | tf_op jit(solution)/shard_map/cond/branch_0_fun/ppermute | solution.py:338
  5.3 6.7 %collective-permute-start.2 = (bf16[8,512]{1,0:T(8,128)(2,1)S(1)}, bf16[8,512]{1,0:T(8,128)(2,1)S(1)}, u32[]{:S(2)}, u32[]{:S(2)}) collective-permute-start(bf16[8,512]{1,0:T(8,128)(2,1)S(1)} %slice.92), channel_id=1, source_target_pairs={{31,0},{28,1},{29,2},{30,3},{3,4},{0,5},{1,6},{2,7},{7,8},{4,9},{5... | collective-permute-start | bytes 24584 | tf_op jit(solution)/shard_map/cond/branch_0_fun/ppermute | solution.py:337
  18.3 7.3 %collective-permute-start.16 = (bf16[48,512]{1,0:T(8,128)(2,1)S(1)}, bf16[48,512]{1,0:T(8,128)(2,1)S(1)}, u32[]{:S(2)}, u32[]{:S(2)}) collective-permute-start(bf16[48,512]{1,0:T(8,128)(2,1)S(1)} %slice.104), channel_id=1, source_target_pairs={{3,0},{0,1},{1,2},{2,3},{7,4},{4,5},{5,6},{6,7},{11,8},{8,9},{9,10... | collective-permute-start | bytes 147464 | tf_op jit(solution)/shard_map/cond/branch_0_fun/ppermute | solution.py:336
  18.4 7.2 %collective-permute-start.15 = (bf16[48,512]{1,0:T(8,128)(2,1)S(1)}, bf16[48,512]{1,0:T(8,128)(2,1)S(1)}, u32[]{:S(2)}, u32[]{:S(2)}) collective-permute-start(bf16[48,512]{1,0:T(8,128)(2,1)S(1)} %slice.103), channel_id=1, source_target_pairs={{28,0},{0,4},{4,8},{8,12},{12,16},{16,20},{20,24},{24,28},{29,1},{... | collective-permute-start | bytes 147464 | tf_op jit(solution)/shard_map/cond/branch_0_fun/ppermute | solution.py:338
  18.5 7.1 %collective-permute-start.17 = (bf16[8,512]{1,0:T(8,128)(2,1)S(1)}, bf16[8,512]{1,0:T(8,128)(2,1)S(1)}, u32[]{:S(2)}, u32[]{:S(2)}) collective-permute-start(bf16[8,512]{1,0:T(8,128)(2,1)S(1)} %slice.105), channel_id=1, source_target_pairs={{31,0},{28,1},{29,2},{30,3},{3,4},{0,5},{1,6},{2,7},{7,8},{4,9},{5... | collective-permute-start | bytes 24584 | tf_op jit(solution)/shard_map/cond/branch_0_fun/ppermute | solution.py:337
  31.0 5.3 %collective-permute-start.47 = (bf16[24,512]{1,0:T(8,128)(2,1)S(1)}, bf16[24,512]{1,0:T(8,128)(2,1)S(1)}, u32[]{:S(2)}, u32[]{:S(2)}) collective-permute-start(bf16[24,512]{1,0:T(8,128)(2,1)S(1)} %slice.131), channel_id=1, source_target_pairs={{5,0},{6,1},{7,2},{4,3},{9,4},{10,5},{11,6},{8,7},{13,8},{14,9},{1... | collective-permute-start | bytes 73736 | tf_op jit(solution)/shard_map/cond/branch_3_fun/ppermute | solution.py:337
  32.8 4.7 %collective-permute-start.46 = (bf16[96,512]{1,0:T(8,128)(2,1)S(1)}, bf16[96,512]{1,0:T(8,128)(2,1)S(1)}, u32[]{:S(2)}, u32[]{:S(2)}) collective-permute-start(bf16[96,512]{1,0:T(8,128)(2,1)S(1)} %slice.130), channel_id=1, source_target_pairs={{1,0},{2,1},{3,2},{0,3},{5,4},{6,5},{7,6},{4,7},{9,8},{10,9},{11,1... | collective-permute-start | bytes 294920 | tf_op jit(solution)/shard_map/cond/branch_3_fun/ppermute | solution.py:336
  33.9 3.6 %collective-permute-start.45 = (bf16[96,512]{1,0:T(8,128)(2,1)S(1)}, bf16[96,512]{1,0:T(8,128)(2,1)S(1)}, u32[]{:S(2)}, u32[]{:S(2)}) collective-permute-start(bf16[96,512]{1,0:T(8,128)(2,1)S(1)} %slice.129), channel_id=1, source_target_pairs={{4,0},{8,4},{12,8},{16,12},{20,16},{24,20},{28,24},{0,28},{5,1},{9... | collective-permute-start | bytes 294920 | tf_op jit(solution)/shard_map/cond/branch_3_fun/ppermute | solution.py:338
where the time goes:
time: 39.2 us; the launch traced here: 39 us
  Pallas kernels  20.8 us (53%)
  starting transfers between devices  11 us (28%)
  waiting for transfers between devices  5.72 us (15%)
  between operations  0.85 us (2%)
  loops' own time  0.58 us (1%)
    pallas_call x9, Pallas kernels, call(): pl.pallas_call(body, out_shape=outs, in_specs=in_specs, out_specs=out_spe...  20.8 us
    ppermute x3, starting transfers between devices, exchange(): both = lax.ppermute(both, ('lat', 'lon'), pairs)  6.12 us
    ppermute x3, waiting for transfers between devices, exchange(): both = lax.ppermute(both, ('lat', 'lon'), pairs)  4.59 us
    ppermute x3, starting transfers between devices, exchange(): col = lax.ppermute(col, 'lon', [((j + sign) % lon, j) for j in range(lon)])  4.25 us
    ppermute x3, waiting for transfers between devices, exchange(): col = lax.ppermute(col, 'lon', [((j + sign) % lon, j) for j in range(lon)])  1.12 us
  transfers between devices with their start and end apart: 9, of which 3 were waited for; matrix products, arithmetic and copies ran while one was open for 0% of the time, Pallas kernels for 17%

commit v1 on v0

--- a/solution.py
+++ b/solution.py
@@ -17,6 +17,7 @@
 SCALE = float(np.log2(np.e) / np.sqrt(HD))
 
 NT = (((1,), (1,)), ((), ()))
+TN = (((0,), (0,)), ((), ()))
 F32 = jnp.float32
 BF16 = jnp.bfloat16
 I32 = jnp.int32
@@ -241,11 +242,12 @@
         v = qkv_of(w, 2 * inner + g * 128)
         values = jnp.concatenate([v, jnp.ones_like(v)], axis=1)
         out = jnp.dot(weights.pop((w, g)), values, preferred_element_type=F32)
-        out = out[:, :128] * (1.0 / out[:, 128:])
-        picked = out[:TOK]
+        picked, total = out[:TOK, :128], out[:TOK, 128:]
         for h in range(1, 4):
-            picked = jnp.where(lane < h * HD, picked, out[h * TOK : (h + 1) * TOK])
-        outs[w, g] = picked.astype(BF16)
+            rows = slice(h * TOK, (h + 1) * TOK)
+            picked = jnp.where(lane < h * HD, picked, out[rows, :128])
+            total = jnp.where(lane < h * HD, total, out[rows, 128:])
+        outs[w, g] = (picked / total).astype(BF16)
         if g == groups - 1:
             finish(w, jnp.concatenate([outs.pop((w, k)) for k in range(groups)], axis=1))
 
@@ -405,7 +407,6 @@
 
     places = np.concatenate([lanes(fine, 1, 1), lanes(coarse, 2, 0)], axis=1)
     lines = places.shape[1]
-    count = 128 * lines
 
     def body(flags_ref, rows_ref, regions_hbm, places_hbm, tokens_hbm, *refs):
         weights_hbm, refs = refs[: len(weights)], refs[len(weights) :]
@@ -426,19 +427,19 @@
         wrapped = jnp.where((row < 0) | (row >= lat), 4.0, 0.0)
         row = jnp.where(row < 0, row + lat, jnp.where(row >= lat, row - lat, row))
         col = jnp.where(col < 0, col + lon, jnp.where(col >= lon, col - lon, col))
-        row = columns_of(row + places_ref[0] * lat, count)
-        col = columns_of(col, count)
-        wrapped = columns_of(wrapped, count)
-        picked = select_rows(row, regions_ref[...].astype(F32).astype(BF16))
-        ids = jnp.zeros((count, 128), F32)
-        for at in range(0, lon, 128):
-            size = min(128, lon - at)
-            lane = lax.broadcasted_iota(I32, (1, size), 1).astype(F32) + float(at)
-            here = jnp.where(lane == col[:, :size], picked[:, at : at + size], 0.0)
-            ids = ids + jnp.sum(here, axis=1, keepdims=True)
-        ids = ids + wrapped
+        row = row + places_ref[0] * lat
+
+        def along(values):
+            return jnp.concatenate([values[n : n + 1] for n in range(lines)], axis=1)
+
+        line = lax.broadcasted_iota(I32, (2 * lat, 1), 0).astype(F32)
+        pick = jnp.where(line == along(row), 1.0, 0.0).astype(BF16)
+        known = regions_ref[...].astype(F32).astype(BF16)
+        picked = lax.dot_general(known, pick, TN, preferred_element_type=F32)
+        line = lax.broadcasted_iota(I32, (lon, 1), 0).astype(F32)
+        ids = jnp.sum(jnp.where(line == along(col), picked, 0.0), axis=0, keepdims=True) + along(wrapped)
         for n in range(lines):
-            id_ref[n : n + 1, :] = ids[n * 128 : (n + 1) * 128].T[:1]
+            id_ref[n : n + 1, :] = ids[:, n * 128 : (n + 1) * 128]
         held.wait()
         take = columns_of(rows_of(plan, rows_ref, "take_one"), len(fine))
         x_ref[...] = select_rows(take, flat(tokens_ref)).astype(BF16)

time: 39.2 us -> 41.2 us (1.051)
  starting transfers between devices: 11 us -> 13.9 us
  Pallas kernels: 20.8 us -> 20.3 us
  waiting for transfers between devices: 5.72 us -> 5.24 us
    ppermute x3, starting transfers between devices: 6.12 us -> 8.22 us  [exchange(): both = lax.ppermute(both, ('lat', 'lon'), pairs)]
    ppermute x3, starting transfers between devices: 0.65 us -> 1.29 us  [exchange(): row = lax.ppermute(row, 'lat', [((i + sign) % lat, i) for i in range(lat)])]
    ppermute x3, waiting for transfers between devices: 4.59 us -> 3.99 us  [exchange(): both = lax.ppermute(both, ('lat', 'lon'), pairs)]
    pallas_call x9, Pallas kernels: 20.8 us -> 20.3 us  [call(): pl.pallas_call(body, out_shape=outs, in_specs=in_specs, out_specs=out_spe...]
  transfers between devices with their start and end apart: 9 -> 9, of which waited for: 3 -> 2; matrix products, arithmetic and copies ran while one was open for 0% -> 0% of each run, Pallas kernels for 17% -> 17%
where the time goes in v1:
time: 41.2 us; the launch traced here: 41 us
  Pallas kernels  20.3 us (49%)
  starting transfers between devices  13.9 us (34%)
  waiting for transfers between devices  5.24 us (13%)
  between operations  0.85 us (2%)
  loops' own time  0.64 us (2%)
    pallas_call x9, Pallas kernels, call(): pl.pallas_call(body, out_shape=outs, in_specs=in_specs, out_specs=out_spe...  20.3 us
    ppermute x3, starting transfers between devices, exchange(): both = lax.ppermute(both, ('lat', 'lon'), pairs)  8.22 us
    ppermute x3, starting transfers between devices, exchange(): col = lax.ppermute(col, 'lon', [((j + sign) % lon, j) for j in range(lon)])  4.36 us
    ppermute x3, waiting for transfers between devices, exchange(): both = lax.ppermute(both, ('lat', 'lon'), pairs)  3.99 us
    ppermute x3, starting transfers between devices, exchange(): row = lax.ppermute(row, 'lat', [((i + sign) % lat, i) for i in range(lat)])  1.29 us
    ppermute x3, waiting for transfers between devices, exchange(): col = lax.ppermute(col, 'lon', [((j + sign) % lon, j) for j in range(lon)])  1.24 us
  transfers between devices with their start and end apart: 9, of which 2 were waited for; matrix products, arithmetic and copies ran while one was open for 0% of the time, Pallas kernels for 17%

profile of v1, /device:TPU:0, one launch (start us, length us, event | category | flops | bytes accessed | tf_op | source)
XLA Modules:
  0.0 41.0 jit_solution(8342145807266132377)
XLA Ops:
  0.6 1.6 %shard_map.116 = (bf16[112,512]{1,0:T(8,128)(2,1)S(1)}, bf16[112,512]{1,0:T(8,128)(2,1)S(1)}, bf16[48,512]{1,0:T(8,128)(2,1)S(1)}, f32[32,128]{1,0:T(8,128)S(1)}...) custom-call(s32[2]{0:T(128)} %shifts_hbm.1, bf16[2,12,24,512]{3,2,1,0:T(8,128)(2,1)} %tokens_hbm.1, ...), custom_call_target="tpu_custom_call" | custom-call | flops 268435456 | bytes 1048576 | tf_op jit(solution)/shard_map/pallas_call | solution.py:275
  2.2 11.6 %conditional.3 = (bf16[272,512]{1,0:T(8,128)(2,1)S(1)}, f32[7,128]{1,0:T(8,128)S(1)}, bf16[576,512]{1,0:T(8,128)(2,1)S(1)}, bf16[512,1536]{1,0:T(8,128)(2,1)S(1)}, bf16[512,512]{1,0:T(8,128)(2,1)S(1)}) conditional(s32[]{:T(128)S(4)} %bitcast.13, (bf16[112,512]{1,0:T(8,128)(2,1)S(1)}, bf16[112,512]{1,0:T(8,128)(2,1)S(1)}, ...), branch_computations={%region_0.0_spmd, %region_1.0_spmd, %region_2.0_spmd, %region_3.0_... | conditional | flops 268435456 | bytes 5619872 | solution.py:356
  2.3 0.5 %collective-permute-start.12 = (bf16[112,512]{1,0:T(8,128)(2,1)S(1)}, bf16[112,512]{1,0:T(8,128)(2,1)S(1)}, u32[]{:S(2)}, u32[]{:S(2)}) collective-permute-start(bf16[112,512]{1,0:T(8,128)(2,1)S(1)} %get-tuple-element.310), channel_id=1, source_target_pairs={{28,0},{0,4},{4,8},{8,12},{12,16},{16,20},{20,24},{24,28},{29,1},{... | collective-permute-start | bytes 344072 | tf_op jit(solution)/shard_map/cond/branch_4_fun/ppermute | solution.py:340
  2.8 2.6 %collective-permute-start.13 = (bf16[112,512]{1,0:T(8,128)(2,1)S(1)}, bf16[112,512]{1,0:T(8,128)(2,1)S(1)}, u32[]{:S(2)}, u32[]{:S(2)}) collective-permute-start(bf16[112,512]{1,0:T(8,128)(2,1)S(1)} %get-tuple-element.311), channel_id=1, source_target_pairs={{3,0},{0,1},{1,2},{2,3},{7,4},{4,5},{5,6},{6,7},{11,8},{8,9},{9,10... | collective-permute-start | bytes 344072 | tf_op jit(solution)/shard_map/cond/branch_4_fun/ppermute | solution.py:338
  5.4 2.4 %collective-permute-start.14 = (bf16[40,512]{1,0:T(8,128)(2,1)S(1)}, bf16[40,512]{1,0:T(8,128)(2,1)S(1)}, u32[]{:S(2)}, u32[]{:S(2)}) collective-permute-start(bf16[40,512]{1,0:T(8,128)(2,1)S(1)} %slice.102), channel_id=1, source_target_pairs={{31,0},{28,1},{29,2},{30,3},{3,4},{0,5},{1,6},{2,7},{7,8},{4,9},{5... | collective-permute-start | bytes 122888 | tf_op jit(solution)/shard_map/cond/branch_4_fun/ppermute | solution.py:339
  7.8 1.9 %branch_4_fun.7 = (f32[7,128]{1,0:T(8,128)S(1)}, bf16[576,512]{1,0:T(8,128)(2,1)S(1)}, bf16[512,1536]{1,0:T(8,128)(2,1)S(1)}, bf16[512,512]{1,0:T(8,128)(2,1)S(1)}) custom-call(s32[8]{0:T(128)S(4)} %get-tuple-element.313.flags_ref, f32[32,128]{1,0:T(8,128)S(1)} %get-tuple-element.314.rows_ref, s32[192,96]{1,0:T(8,128)} %bitcast.18, ...), custom_call_target="tpu_custom_call" | custom-call | flops 268435456 | bytes 4194304 | tf_op jit(solution)/shard_map/cond/branch_4_fun/pallas_call | solution.py:275
  9.7 4.0 %collective-permute-done.14.refs_2_ = bf16[40,512]{1,0:T(8,128)(2,1)S(1)} collective-permute-done((bf16[40,512]{1,0:T(8,128)(2,1)S(1)}, bf16[40,512]{1,0:T(8,128)(2,1)S(1)}, u32[]{:S(2)}, u32[]{:S(2)}) %collective-permute-start.14) | collective-permute-done | bytes 40992 | tf_op jit(solution)/shard_map/cond/branch_4_fun/ppermute | solution.py:339
  13.7 0.0 collective-permute-done.12.refs_0_
  13.7 0.0 collective-permute-done.13.refs_1_
  13.8 5.9 %shard_map.117 = (bf16[576,512]{1,0:T(8,128)(2,1)}, bf16[160,512]{1,0:T(8,128)(2,1)S(1)}, bf16[160,512]{1,0:T(8,128)(2,1)S(1)}, bf16[112,512]{1,0:T(8,128)(2,1)S(1)}) custom-call(bf16[576,512]{1,0:T(8,128)(2,1)S(1)} %get-tuple-element.469.own_ref, bf16[272,512]{1,0:T(8,128)(2,1)S(1)} %get-tuple-element.470.source_ref, ...), custom_call_target="tpu_custom_call" | custom-call | flops 3221225472 | bytes 6291456 | tf_op jit(solution)/shard_map/pallas_call | solution.py:275
  19.7 6.0 %conditional.4 = (bf16[432,512]{1,0:T(8,128)(2,1)S(1)}, bf16[576,512]{1,0:T(8,128)(2,1)S(1)}, bf16[576,512]{1,0:T(8,128)(2,1)}, bf16[768,1024]{1,0:T(8,128)(2,1)S(1)}) conditional(s32[]{:T(128)S(4)} %bitcast.12, (bf16[160,512]{1,0:T(8,128)(2,1)S(1)}, bf16[160,512]{1,0:T(8,128)(2,1)S(1)}, ...), branch_computations={%region_5.0_spmd, %region_6.0_spmd, %region_7.0_spmd, %region_8.0_... | conditional | flops 268435456 | bytes 6619288 | solution.py:356
  19.9 1.7 %collective-permute-start.25 = (bf16[120,512]{1,0:T(8,128)(2,1)S(1)}, bf16[120,512]{1,0:T(8,128)(2,1)S(1)}, u32[]{:S(2)}, u32[]{:S(2)}) collective-permute-start(bf16[120,512]{1,0:T(8,128)(2,1)S(1)} %slice.113), channel_id=1, source_target_pairs={{1,0},{2,1},{3,2},{0,3},{5,4},{6,5},{7,6},{4,7},{9,8},{10,9},{11,1... | collective-permute-start | bytes 368648 | tf_op jit(solution)/shard_map/cond/branch_3_fun/ppermute | solution.py:338
  21.6 0.4 %collective-permute-start.24 = (bf16[120,512]{1,0:T(8,128)(2,1)S(1)}, bf16[120,512]{1,0:T(8,128)(2,1)S(1)}, u32[]{:S(2)}, u32[]{:S(2)}) collective-permute-start(bf16[120,512]{1,0:T(8,128)(2,1)S(1)} %slice.112), channel_id=1, source_target_pairs={{4,0},{8,4},{12,8},{16,12},{20,16},{24,20},{28,24},{0,28},{5,1},{9... | collective-permute-start | bytes 368648 | tf_op jit(solution)/shard_map/cond/branch_3_fun/ppermute | solution.py:340
  22.1 0.9 %collective-permute-start.26 = (bf16[40,512]{1,0:T(8,128)(2,1)S(1)}, bf16[40,512]{1,0:T(8,128)(2,1)S(1)}, u32[]{:S(2)}, u32[]{:S(2)}) collective-permute-start(bf16[40,512]{1,0:T(8,128)(2,1)S(1)} %slice.114), channel_id=1, source_target_pairs={{5,0},{6,1},{7,2},{4,3},{9,4},{10,5},{11,6},{8,7},{13,8},{14,9},{1... | collective-permute-start | bytes 122888 | tf_op jit(solution)/shard_map/cond/branch_3_fun/ppermute | solution.py:339
  23.0 2.6 %branch_3_fun.9 = (bf16[576,512]{1,0:T(8,128)(2,1)S(1)}, bf16[576,512]{1,0:T(8,128)(2,1)}, bf16[768,1024]{1,0:T(8,128)(2,1)S(1)}) custom-call(f32[32,128]{1,0:T(8,128)S(1)} %get-tuple-element.353.rows_ref, bf16[576,512]{1,0:T(8,128)(2,1)} %get-tuple-element.354.fine_hbm, bf16[2048,1024]{1,0:T(8,128)(2,1)} %get-tuple-element.355.weight_hbm), custom_call_target="tpu_custom_call" | custom-call | flops 268435456 | bytes 4194304 | tf_op jit(solution)/shard_map/cond/branch_3_fun/pallas_call | solution.py:275
  25.6 0.0 collective-permute-done.26.refs_2_
  25.6 0.0 collective-permute-done.25.refs_1_
  25.6 0.0 collective-permute-done.24.refs_0_
  25.7 4.8 %shard_map.118 = (bf16[144,1024]{1,0:T(8,128)(2,1)S(1)}, bf16[128,512]{1,0:T(8,128)(2,1)S(1)}, bf16[128,512]{1,0:T(8,128)(2,1)S(1)}, bf16[88,512]{1,0:T(8,128)(2,1)S(1)}) custom-call(s32[8]{0:T(128)S(4)} %get-tuple-element.467.flags_ref, bf16[576,512]{1,0:T(8,128)(2,1)} %get-tuple-element.477.fine_hbm, bf16[2048,1024]{1,0:T(8,128)(2,1)} %merge_hbm.1, ...), custom_call_target="tpu_custom_call" | custom-call | flops 3221225472 | bytes 12582912 | tf_op jit(solution)/shard_map/pallas_call | solution.py:275
  30.4 10.3 %conditional.5 = (bf16[2,12,24,512]{3,2,1,0:T(8,128)(2,1)}, bf16[2,6,12,1024]{3,0,2,1:T(2,128)(2,1)}) conditional(s32[]{:T(128)S(4)} %bitcast.11, (bf16[576,512]{1,0:T(8,128)(2,1)}, bf16[432,512]{1,0:T(8,128)(2,1)S(1)}, f32[32,128]{1,0:T(8,128)S(1)}, bf16[128,512]{1,0:T(8,128)(2,1)S(1)}, ...), branch_computations={%region_12.0_spmd, %region_13.0_spmd, %region_14.0_spmd, %region_1... | conditional | flops 1342177280 | bytes 6865032 | solution.py:356
  30.5 4.9 %collective-permute-start.41 = (bf16[16,512]{1,0:T(8,128)(2,1)S(1)}, bf16[16,512]{1,0:T(8,128)(2,1)S(1)}, u32[]{:S(2)}, u32[]{:S(2)}) collective-permute-start(bf16[16,512]{1,0:T(8,128)(2,1)S(1)} %slice.125), channel_id=1, source_target_pairs={{5,0},{6,1},{7,2},{4,3},{9,4},{10,5},{11,6},{8,7},{13,8},{14,9},{1... | collective-permute-start | bytes 49160 | tf_op jit(solution)/shard_map/cond/branch_1_fun/ppermute | solution.py:339
  35.4 0.0 collective-permute-start.40
  35.4 0.4 collective-permute-start.39
  35.7 2.5 %branch_1_fun.10 = bf16[2,12,24,512]{3,2,1,0:T(8,128)(2,1)} custom-call(bf16[576,512]{1,0:T(8,128)(2,1)} %get-tuple-element.393.part_hbm, bf16[432,512]{1,0:T(8,128)(2,1)S(1)} %get-tuple-element.394.source_ref, f32[32,128]{1,0:T(8,128)S(1)} %get-tuple-element.395.rows_ref.refs_3_), custom_call_target="tpu_custom_call" | custom-call | flops 1073741824 | bytes 4194304 | tf_op jit(solution)/shard_map/cond/branch_1_fun/pallas_call | solution.py:275
  38.2 0.0 collective-permute-done.41.refs_2_
  38.2 1.2 %collective-permute-done.40.refs_1_ = bf16[48,512]{1,0:T(8,128)(2,1)S(1)} collective-permute-done((bf16[48,512]{1,0:T(8,128)(2,1)S(1)}, bf16[48,512]{1,0:T(8,128)(2,1)S(1)}, u32[]{:S(2)}, u32[]{:S(2)}) %collective-permute-start.40) | collective-permute-done | bytes 49184 | tf_op jit(solution)/shard_map/cond/branch_1_fun/ppermute | solution.py:338
  39.4 0.0 collective-permute-done.39.refs_0_
  39.4 1.1 %branch_1_fun.11 = bf16[6,12,2,1024]{3,2,1,0:T(2,128)(2,1)} custom-call(bf16[144,1024]{1,0:T(8,128)(2,1)S(1)} %get-tuple-element.396.coarse_ref, bf16[48,512]{1,0:T(8,128)(2,1)S(1)} %collective-permute-done.39.refs_0_, bf16[48,512]{1,0:T(8,128)(2,1)S(1)} %collective-permute-done.40.refs_1_, bf16[16,512]{1,0:T(8,128)(2,1)S(1)} %collective-permute-done.41.refs_2_, ...), custom_call_target="tpu_custom_call" | custom-call | flops 268435456 | bytes 1048576 | tf_op jit(solution)/shard_map/cond/branch_1_fun/pallas_call | solution.py:275
  (9 shorter events, 0.1 us)
Async XLA Ops:
  2.3 11.5 %collective-permute-start.12 = (bf16[112,512]{1,0:T(8,128)(2,1)S(1)}, bf16[112,512]{1,0:T(8,128)(2,1)S(1)}, u32[]{:S(2)}, u32[]{:S(2)}) collective-permute-start(bf16[112,512]{1,0:T(8,128)(2,1)S(1)} %get-tuple-element.310), channel_id=1, source_target_pairs={{28,0},{0,4},{4,8},{8,12},{12,16},{16,20},{20,24},{24,28},{29,1},{... | collective-permute-start | bytes 344072 | tf_op jit(solution)/shard_map/cond/branch_4_fun/ppermute | solution.py:340
  2.8 11.0 %collective-permute-start.13 = (bf16[112,512]{1,0:T(8,128)(2,1)S(1)}, bf16[112,512]{1,0:T(8,128)(2,1)S(1)}, u32[]{:S(2)}, u32[]{:S(2)}) collective-permute-start(bf16[112,512]{1,0:T(8,128)(2,1)S(1)} %get-tuple-element.311), channel_id=1, source_target_pairs={{3,0},{0,1},{1,2},{2,3},{7,4},{4,5},{5,6},{6,7},{11,8},{8,9},{9,10... | collective-permute-start | bytes 344072 | tf_op jit(solution)/shard_map/cond/branch_4_fun/ppermute | solution.py:338
  5.4 8.3 %collective-permute-start.14 = (bf16[40,512]{1,0:T(8,128)(2,1)S(1)}, bf16[40,512]{1,0:T(8,128)(2,1)S(1)}, u32[]{:S(2)}, u32[]{:S(2)}) collective-permute-start(bf16[40,512]{1,0:T(8,128)(2,1)S(1)} %slice.102), channel_id=1, source_target_pairs={{31,0},{28,1},{29,2},{30,3},{3,4},{0,5},{1,6},{2,7},{7,8},{4,9},{5... | collective-permute-start | bytes 122888 | tf_op jit(solution)/shard_map/cond/branch_4_fun/ppermute | solution.py:339
  19.9 5.7 %collective-permute-start.25 = (bf16[120,512]{1,0:T(8,128)(2,1)S(1)}, bf16[120,512]{1,0:T(8,128)(2,1)S(1)}, u32[]{:S(2)}, u32[]{:S(2)}) collective-permute-start(bf16[120,512]{1,0:T(8,128)(2,1)S(1)} %slice.113), channel_id=1, source_target_pairs={{1,0},{2,1},{3,2},{0,3},{5,4},{6,5},{7,6},{4,7},{9,8},{10,9},{11,1... | collective-permute-start | bytes 368648 | tf_op jit(solution)/shard_map/cond/branch_3_fun/ppermute | solution.py:338
  21.6 4.0 %collective-permute-start.24 = (bf16[120,512]{1,0:T(8,128)(2,1)S(1)}, bf16[120,512]{1,0:T(8,128)(2,1)S(1)}, u32[]{:S(2)}, u32[]{:S(2)}) collective-permute-start(bf16[120,512]{1,0:T(8,128)(2,1)S(1)} %slice.112), channel_id=1, source_target_pairs={{4,0},{8,4},{12,8},{16,12},{20,16},{24,20},{28,24},{0,28},{5,1},{9... | collective-permute-start | bytes 368648 | tf_op jit(solution)/shard_map/cond/branch_3_fun/ppermute | solution.py:340
  22.1 3.5 %collective-permute-start.26 = (bf16[40,512]{1,0:T(8,128)(2,1)S(1)}, bf16[40,512]{1,0:T(8,128)(2,1)S(1)}, u32[]{:S(2)}, u32[]{:S(2)}) collective-permute-start(bf16[40,512]{1,0:T(8,128)(2,1)S(1)} %slice.114), channel_id=1, source_target_pairs={{5,0},{6,1},{7,2},{4,3},{9,4},{10,5},{11,6},{8,7},{13,8},{14,9},{1... | collective-permute-start | bytes 122888 | tf_op jit(solution)/shard_map/cond/branch_3_fun/ppermute | solution.py:339
  30.5 7.7 %collective-permute-start.41 = (bf16[16,512]{1,0:T(8,128)(2,1)S(1)}, bf16[16,512]{1,0:T(8,128)(2,1)S(1)}, u32[]{:S(2)}, u32[]{:S(2)}) collective-permute-start(bf16[16,512]{1,0:T(8,128)(2,1)S(1)} %slice.125), channel_id=1, source_target_pairs={{5,0},{6,1},{7,2},{4,3},{9,4},{10,5},{11,6},{8,7},{13,8},{14,9},{1... | collective-permute-start | bytes 49160 | tf_op jit(solution)/shard_map/cond/branch_1_fun/ppermute | solution.py:339
  35.4 4.1 %collective-permute-start.40 = (bf16[48,512]{1,0:T(8,128)(2,1)S(1)}, bf16[48,512]{1,0:T(8,128)(2,1)S(1)}, u32[]{:S(2)}, u32[]{:S(2)}) collective-permute-start(bf16[48,512]{1,0:T(8,128)(2,1)S(1)} %slice.124), channel_id=1, source_target_pairs={{1,0},{2,1},{3,2},{0,3},{5,4},{6,5},{7,6},{4,7},{9,8},{10,9},{11,1... | collective-permute-start | bytes 147464 | tf_op jit(solution)/shard_map/cond/branch_1_fun/ppermute | solution.py:338
  35.4 4.1 %collective-permute-start.39 = (bf16[48,512]{1,0:T(8,128)(2,1)S(1)}, bf16[48,512]{1,0:T(8,128)(2,1)S(1)}, u32[]{:S(2)}, u32[]{:S(2)}) collective-permute-start(bf16[48,512]{1,0:T(8,128)(2,1)S(1)} %slice.123), channel_id=1, source_target_pairs={{4,0},{8,4},{12,8},{16,12},{20,16},{24,20},{28,24},{0,28},{5,1},{9... | collective-permute-start | bytes 147464 | tf_op jit(solution)/shard_map/cond/branch_1_fun/ppermute | solution.py:340

commit v2 on v1

--- a/solution.py
+++ b/solution.py
@@ -216,40 +216,39 @@
     return values * lax.rsqrt(spread + EPS)
 
 
-def attend_windows(qkv_of, id_of, windows, inner, finish):
-    lane = lax.broadcasted_iota(I32, (1, 128), 1)
-    forbid = jnp.where(lane < 8, BIG, 0.0).astype(BF16)
-    groups = inner // 128
-    units = [(w, g) for w in range(windows) for g in range(groups)]
+def attend_windows(qkv_of, key_ids, query_ids, windows, inner, finish):
+    lane = lax.broadcasted_iota(I32, (1, 256), 1)
+    units = [(w, g) for w in range(windows) for g in range(inner // 256)]
     scores, weights, outs = {}, {}, {}
 
     def score(w, g):
-        key_id = id_of(w)
-        not_id = (key_id - 1).astype(BF16) * forbid
-        q = qkv_of(w, g * 128)
-        keys = jnp.concatenate([qkv_of(w, inner + g * 128), key_id], axis=1)
-        queries = []
-        for h in range(4):
-            mine = jnp.where((lane >= h * HD) & (lane < (h + 1) * HD), 1.0, 0.0).astype(BF16)
-            queries.append(jnp.concatenate([q * mine, not_id], axis=1))
-        scores[w, g] = lax.dot_general(stack_rows(queries), keys, NT, preferred_element_type=F32)
+        q, k = qkv_of(w, g * 256), qkv_of(w, inner + g * 256)
+        masks = [jnp.where((lane >= h * HD) & (lane < (h + 1) * HD), 1.0, 0.0).astype(BF16) for h in range(8)]
+        queries = stack_rows([q * mine for mine in masks])
+        scores[w, g] = lax.dot_general(k, queries, NT, preferred_element_type=F32)
 
     def soften(w, g):
-        s = scores.pop((w, g))
-        weights[w, g] = jnp.exp2((s - jnp.max(s, axis=1, keepdims=True)) * SCALE).astype(BF16)
+        s = jnp.where(key_ids(w) == query_ids(w), scores.pop((w, g)), -BIG)
+        weight = jnp.exp2((s - jnp.max(s, axis=0, keepdims=True)) * SCALE)
+        weights[w, g] = weight.astype(BF16), 1.0 / jnp.sum(weight, axis=0, keepdims=True)
 
     def gather(w, g):
-        v = qkv_of(w, 2 * inner + g * 128)
-        values = jnp.concatenate([v, jnp.ones_like(v)], axis=1)
-        out = jnp.dot(weights.pop((w, g)), values, preferred_element_type=F32)
-        picked, total = out[:TOK, :128], out[:TOK, 128:]
-        for h in range(1, 4):
-            rows = slice(h * TOK, (h + 1) * TOK)
-            picked = jnp.where(lane < h * HD, picked, out[rows, :128])
-            total = jnp.where(lane < h * HD, total, out[rows, 128:])
-        outs[w, g] = (picked / total).astype(BF16)
-        if g == groups - 1:
-            finish(w, jnp.concatenate([outs.pop((w, k)) for k in range(groups)], axis=1))
+        weight, scale = weights.pop((w, g))
+        values = qkv_of(w, 2 * inner + g * 256).T
+        parts = []
+        for at in range(0, 8 * TOK, 256):
+            end = min(at + 256, 8 * TOK)
+            first, last = at // TOK, (end - 1) // TOK
+            out = jnp.dot(values[first * HD : (last + 1) * HD], weight[:, at:end], preferred_element_type=F32)
+            picked = out[:HD]
+            for h in range(first + 1, last + 1):
+                mine = out[(h - first) * HD : (h - first + 1) * HD]
+                picked = jnp.where(lane[:, : end - at] < h * TOK - at, picked, mine)
+            parts.append(picked)
+        out = (jnp.concatenate(parts, axis=1) * scale).astype(BF16)
+        outs[w, g] = [out[:, h * TOK : (h + 1) * TOK] for h in range(8)]
+        if g == inner // 256 - 1:
+            finish(w, stack_rows([part for k in range(inner // 256) for part in outs.pop((w, k))]))
 
     for n in range(len(units) + 2):
         if n < len(units):
@@ -455,9 +454,9 @@
     return ids, x, weights
 
 
-def id_columns(lines, count):
-    lane = lax.broadcasted_iota(I32, (1, 128), 1).astype(F32)
-    return jnp.where(columns_of(lines, count) == lane, 1.0, 0.0).astype(BF16)
+def along_lanes(lines, at):
+    flat_lines = jnp.concatenate([lines[n : n + 1] for n in range(lines.shape[0])], axis=1)
+    return jnp.concatenate([flat_lines[:, at : at + TOK]] * 8, axis=1)
 
 
 def before_coarse(fine, table, weight, plan):
@@ -489,7 +488,8 @@
     def body(own_ref, source_ref, ids_ref, qkv_w_ref, proj_w_ref, rows_ref, out_hbm, *refs):
         *piece_outs, x_ref, qkv_ref, out_ref, id_ref, sems = refs
         start = Copies(sems)
-        id_ref[...] = id_columns(ids_ref[: -(-count // 128), :], count)
+        lines = ids_ref[: -(-count // 128), :]
+        id_ref[...] = columns_of(lines, count)
         leave = []
         take = columns_of(rows_of(plan, rows_ref, "take_one"), count) - float(count)
         x = own_ref[...].astype(F32) + select_rows(take, source_ref[...])
@@ -499,13 +499,14 @@
 
         def finish(w, out):
             at = slice(w * TOK, (w + 1) * TOK)
-            out = jnp.dot(out, proj_w_ref[...], preferred_element_type=F32)
+            out = lax.dot_general(out, proj_w_ref[...], TN, preferred_element_type=F32)
             out_ref[at, :] = (x_ref[at, :] + out).astype(BF16)
             leave.append(start(out_ref.at[pl.ds(w * TOK, TOK)], out_hbm.at[pl.ds(w * TOK, TOK)]))
 
         attend_windows(
-            lambda w, at: qkv_ref[w * TOK : (w + 1) * TOK, at : at + 128],
-            lambda w: id_ref[w * TOK : (w + 1) * TOK, :],
+            lambda w, at: qkv_ref[w * TOK : (w + 1) * TOK, at : at + 256],
+            lambda w: id_ref[w * TOK : (w + 1) * TOK, :1],
+            lambda w: along_lanes(lines, w * TOK),
             count // TOK,
             inner,
             finish,
@@ -520,7 +521,7 @@
         pltpu.VMEM((count, width), F32),
         pltpu.VMEM((count, 3 * inner), BF16),
         pltpu.VMEM((count, width), BF16),
-        pltpu.VMEM((count, 128), BF16),
+        pltpu.VMEM((count, 128), F32),
     ]
     args = [x_own, source, ids, w_qkv, w_proj, rows]
     out, *sent = call(body, outs, args, [VMEM] * len(args), scratch, count // TOK, 3 << 30, 6 << 20, 14)
@@ -537,7 +538,7 @@
         flags_ref, fine_hbm, merge_hbm, qkv_w_hbm, proj_w_hbm, own_ref, source_ref, ids_ref, first_ref, rows_ref, *refs
     ):
         out_ref, *piece_outs = refs[:4]
-        qkv_ref, fine_ref, id_ref, merge_ref, qkv_w_ref, proj_w_ref, sems = refs[4:]
+        qkv_ref, id_ref, fine_ref, merge_ref, qkv_w_ref, proj_w_ref, sems = refs[4:]
         start = Copies(sems)
         with_fine = [n for n, sizes in enumerate(plan.four) if sum(sizes)]
         needs_fine = functools.reduce(jnp.logical_or, [flags_ref[0] == n for n in with_fine])
@@ -563,7 +564,8 @@
         def _():
             pltpu.make_async_copy(*fine_copy).start()
 
-        id_ref[...] = id_columns(ids_ref[-(-own // 128) :, :], count)
+        lines = ids_ref[-(-own // 128) :, :]
+        id_ref[...] = columns_of(lines, count)
         take = columns_of(rows_of(plan, rows_ref, "take_two"), 4 * count) - float(own)
         x = own_ref[...].astype(F32) + select_rows(take, source_ref[...])
         x = jnp.concatenate([x[n * count : (n + 1) * count] for n in range(4)], axis=1)
@@ -575,10 +577,17 @@
         proj_w.wait()
 
         def finish(w, out):
-            out = jnp.dot(out, proj_w_ref[...], preferred_element_type=F32)
+            out = lax.dot_general(out, proj_w_ref[...], TN, preferred_element_type=F32)
             out_ref[...] = (merged + out).astype(BF16)
 
-        attend_windows(lambda w, at: qkv_ref[:, at : at + 128], lambda w: id_ref[...], 1, inner, finish)
+        attend_windows(
+            lambda w, at: qkv_ref[:, at : at + 256],
+            lambda w: id_ref[:, :1],
+            lambda w: along_lanes(lines, 0),
+            1,
+            inner,
+            finish,
+        )
         sent = select_rows(columns_of(rows_of(plan, rows_ref, "send_three"), sum(plan.room_three)), out_ref[...])
         sent = sent.astype(BF16)
         for n, sizes in enumerate(plan.three):
@@ -607,8 +616,8 @@
 
     most = [max(2 * three[k] + four[k] for three, four in zip(plan.three, plan.four)) for k in range(3)]
     outs = shapes([count], width) + shapes(most, half)
-    scratch = [pltpu.VMEM((count, 3 * inner), BF16)]
-    shapes_in = [fine.shape, (count, 128), (depth - merge_first.shape[0], width), w_qkv.shape, w_proj.shape]
+    scratch = [pltpu.VMEM((count, 3 * inner), BF16), pltpu.VMEM((count, 128), F32)]
+    shapes_in = [fine.shape, (depth - merge_first.shape[0], width), w_qkv.shape, w_proj.shape]
     scratch += [pltpu.VMEM(shape, BF16) for shape in shapes_in]
     args = [flags, fine, w_merge, w_qkv, w_proj, x_own, source, ids, merge_first, rows]
     in_specs = [SMEM] + [HBM] * 4 + [VMEM] * (len(args) - 5)

time: 41.2 us -> 41.6 us (level)
  starting transfers between devices: 13.9 us -> 10.5 us
  waiting for transfers between devices: 5.24 us -> 7.8 us
  Pallas kernels: 20.3 us -> 21.6 us
    ppermute x3, starting transfers between devices: 8.22 us -> 1.66 us  [exchange(): both = lax.ppermute(both, ('lat', 'lon'), pairs)]
    ppermute x3, waiting for transfers between devices: 3.99 us -> 6.8 us  [exchange(): both = lax.ppermute(both, ('lat', 'lon'), pairs)]
    ppermute x3, starting transfers between devices: 4.36 us -> 7.01 us  [exchange(): col = lax.ppermute(col, 'lon', [((j + sign) % lon, j) for j in range(lon)])]
    pallas_call x9, Pallas kernels: 20.3 us -> 21.6 us  [call(): pl.pallas_call(body, out_shape=outs, in_specs=in_specs, out_specs=out_spe...]
    ppermute x3, starting transfers between devices: 1.29 us -> 1.87 us  [exchange(): row = lax.ppermute(row, 'lat', [((i + sign) % lat, i) for i in range(lat)])]
  transfers between devices with their start and end apart: 9 -> 9, of which waited for: 2 -> 3; matrix products, arithmetic and copies ran while one was open for 0% -> 0% of each run, Pallas kernels for 17% -> 17%
where the time goes in v2:
time: 41.6 us; the launch traced here: 41.4 us
  Pallas kernels  21.6 us (52%)
  starting transfers between devices  10.5 us (25%)
  waiting for transfers between devices  7.8 us (19%)
  between operations  0.85 us (2%)
  loops' own time  0.64 us (2%)
    pallas_call x9, Pallas kernels, call(): pl.pallas_call(body, out_shape=outs, in_specs=in_specs, out_specs=out_spe...  21.6 us
    ppermute x3, starting transfers between devices, exchange(): col = lax.ppermute(col, 'lon', [((j + sign) % lon, j) for j in range(lon)])  7.01 us
    ppermute x3, waiting for transfers between devices, exchange(): both = lax.ppermute(both, ('lat', 'lon'), pairs)  6.8 us
    ppermute x3, starting transfers between devices, exchange(): row = lax.ppermute(row, 'lat', [((i + sign) % lat, i) for i in range(lat)])  1.87 us
    ppermute x3, starting transfers between devices, exchange(): both = lax.ppermute(both, ('lat', 'lon'), pairs)  1.66 us
    ppermute x3, waiting for transfers between devices, exchange(): col = lax.ppermute(col, 'lon', [((j + sign) % lon, j) for j in range(lon)])  0.99 us
  transfers between devices with their start and end apart: 9, of which 3 were waited for; matrix products, arithmetic and copies ran while one was open for 0% of the time, Pallas kernels for 17%

profile of v2, /device:TPU:0, one launch (start us, length us, event | category | flops | bytes accessed | tf_op | source)
XLA Modules:
  0.0 41.4 jit_solution(7264080021516945230)
XLA Ops:
  0.6 1.6 %shard_map.116 = (bf16[112,512]{1,0:T(8,128)(2,1)S(1)}, bf16[112,512]{1,0:T(8,128)(2,1)S(1)}, bf16[48,512]{1,0:T(8,128)(2,1)S(1)}, f32[32,128]{1,0:T(8,128)S(1)}...) custom-call(s32[2]{0:T(128)} %shifts_hbm.1, bf16[2,12,24,512]{3,2,1,0:T(8,128)(2,1)} %tokens_hbm.1, ...), custom_call_target="tpu_custom_call" | custom-call | flops 268435456 | bytes 1048576 | tf_op jit(solution)/shard_map/pallas_call | solution.py:274
  2.2 10.0 %conditional.3 = (bf16[272,512]{1,0:T(8,128)(2,1)S(1)}, f32[7,128]{1,0:T(8,128)S(1)}, bf16[576,512]{1,0:T(8,128)(2,1)S(1)}, bf16[512,1536]{1,0:T(8,128)(2,1)S(1)}, bf16[512,512]{1,0:T(8,128)(2,1)S(1)}) conditional(s32[]{:T(128)S(4)} %bitcast.13, (bf16[112,512]{1,0:T(8,128)(2,1)S(1)}, bf16[112,512]{1,0:T(8,128)(2,1)S(1)}, ...), branch_computations={%region_0.0_spmd, %region_1.0_spmd, %region_2.0_spmd, %region_3.0_... | conditional | flops 268435456 | bytes 5619872 | solution.py:355
  2.3 5.1 %collective-permute-start.10 = (bf16[80,512]{1,0:T(8,128)(2,1)S(1)}, bf16[80,512]{1,0:T(8,128)(2,1)S(1)}, u32[]{:S(2)}, u32[]{:S(2)}) collective-permute-start(bf16[80,512]{1,0:T(8,128)(2,1)S(1)} %slice.100), channel_id=1, source_target_pairs={{1,0},{2,1},{3,2},{0,3},{5,4},{6,5},{7,6},{4,7},{9,8},{10,9},{11,1... | collective-permute-start | bytes 245768 | tf_op jit(solution)/shard_map/cond/branch_3_fun/ppermute | solution.py:337
  7.4 1.6 %collective-permute-start.9 = (bf16[80,512]{1,0:T(8,128)(2,1)S(1)}, bf16[80,512]{1,0:T(8,128)(2,1)S(1)}, u32[]{:S(2)}, u32[]{:S(2)}) collective-permute-start(bf16[80,512]{1,0:T(8,128)(2,1)S(1)} %slice.99), channel_id=1, source_target_pairs={{4,0},{8,4},{12,8},{16,12},{20,16},{24,20},{28,24},{0,28},{5,1},{9... | collective-permute-start | bytes 245768 | tf_op jit(solution)/shard_map/cond/branch_3_fun/ppermute | solution.py:339
  9.0 0.8 %collective-permute-start.11 = (bf16[16,512]{1,0:T(8,128)(2,1)S(1)}, bf16[16,512]{1,0:T(8,128)(2,1)S(1)}, u32[]{:S(2)}, u32[]{:S(2)}) collective-permute-start(bf16[16,512]{1,0:T(8,128)(2,1)S(1)} %slice.101), channel_id=1, source_target_pairs={{5,0},{6,1},{7,2},{4,3},{9,4},{10,5},{11,6},{8,7},{13,8},{14,9},{1... | collective-permute-start | bytes 49160 | tf_op jit(solution)/shard_map/cond/branch_3_fun/ppermute | solution.py:338
  9.8 1.9 %branch_3_fun.7 = (f32[7,128]{1,0:T(8,128)S(1)}, bf16[576,512]{1,0:T(8,128)(2,1)S(1)}, bf16[512,1536]{1,0:T(8,128)(2,1)S(1)}, bf16[512,512]{1,0:T(8,128)(2,1)S(1)}) custom-call(s32[8]{0:T(128)S(4)} %get-tuple-element.300.flags_ref, f32[32,128]{1,0:T(8,128)S(1)} %get-tuple-element.301.rows_ref, s32[192,96]{1,0:T(8,128)} %bitcast.17, ...), custom_call_target="tpu_custom_call" | custom-call | flops 268435456 | bytes 4194304 | tf_op jit(solution)/shard_map/cond/branch_3_fun/pallas_call | solution.py:274
  11.7 0.4 %collective-permute-done.11.refs_2_ = bf16[16,512]{1,0:T(8,128)(2,1)S(1)} collective-permute-done((bf16[16,512]{1,0:T(8,128)(2,1)S(1)}, bf16[16,512]{1,0:T(8,128)(2,1)S(1)}, u32[]{:S(2)}, u32[]{:S(2)}) %collective-permute-start.11) | collective-permute-done | bytes 16416 | tf_op jit(solution)/shard_map/cond/branch_3_fun/ppermute | solution.py:338
  12.1 0.0 collective-permute-done.10.refs_1_
  12.1 0.0 collective-permute-done.9.refs_0_
  12.2 6.3 %shard_map.117 = (bf16[576,512]{1,0:T(8,128)(2,1)}, bf16[160,512]{1,0:T(8,128)(2,1)S(1)}, bf16[160,512]{1,0:T(8,128)(2,1)S(1)}, bf16[112,512]{1,0:T(8,128)(2,1)S(1)}) custom-call(bf16[576,512]{1,0:T(8,128)(2,1)S(1)} %get-tuple-element.469.own_ref, bf16[272,512]{1,0:T(8,128)(2,1)S(1)} %get-tuple-element.470.source_ref, ...), custom_call_target="tpu_custom_call" | custom-call | flops 3221225472 | bytes 6291456 | tf_op jit(solution)/shard_map/pallas_call | solution.py:274
  18.5 10.6 %conditional.4 = (bf16[432,512]{1,0:T(8,128)(2,1)S(1)}, bf16[576,512]{1,0:T(8,128)(2,1)S(1)}, bf16[576,512]{1,0:T(8,128)(2,1)}, bf16[768,1024]{1,0:T(8,128)(2,1)S(1)}) conditional(s32[]{:T(128)S(4)} %bitcast.12, (bf16[160,512]{1,0:T(8,128)(2,1)S(1)}, bf16[160,512]{1,0:T(8,128)(2,1)S(1)}, ...), branch_computations={%region_5.0_spmd, %region_6.0_spmd, %region_7.0_spmd, %region_8.0_... | conditional | flops 268435456 | bytes 6619288 | solution.py:355
  18.7 1.2 %collective-permute-start.28 = (bf16[144,512]{1,0:T(8,128)(2,1)S(1)}, bf16[144,512]{1,0:T(8,128)(2,1)S(1)}, u32[]{:S(2)}, u32[]{:S(2)}) collective-permute-start(bf16[144,512]{1,0:T(8,128)(2,1)S(1)} %slice.116), channel_id=1, source_target_pairs={{3,0},{0,1},{1,2},{2,3},{7,4},{4,5},{5,6},{6,7},{11,8},{8,9},{9,10... | collective-permute-start | bytes 442376 | tf_op jit(solution)/shard_map/cond/branch_4_fun/ppermute | solution.py:337
  20.0 0.1 collective-permute-start.27
  20.0 0.1 collective-permute-start.29
  20.1 2.6 %branch_4_fun.9 = (bf16[576,512]{1,0:T(8,128)(2,1)S(1)}, bf16[576,512]{1,0:T(8,128)(2,1)}, bf16[768,1024]{1,0:T(8,128)(2,1)S(1)}) custom-call(f32[32,128]{1,0:T(8,128)S(1)} %get-tuple-element.362.rows_ref, bf16[576,512]{1,0:T(8,128)(2,1)} %get-tuple-element.363.fine_hbm, bf16[2048,1024]{1,0:T(8,128)(2,1)} %get-tuple-element.364.weight_hbm), custom_call_target="tpu_custom_call" | custom-call | flops 268435456 | bytes 4194304 | tf_op jit(solution)/shard_map/cond/branch_4_fun/pallas_call | solution.py:274
  22.7 6.4 %collective-permute-done.29.refs_2_ = bf16[64,512]{1,0:T(8,128)(2,1)S(1)} collective-permute-done((bf16[64,512]{1,0:T(8,128)(2,1)S(1)}, bf16[64,512]{1,0:T(8,128)(2,1)S(1)}, u32[]{:S(2)}, u32[]{:S(2)}) %collective-permute-start.29) | collective-permute-done | bytes 65568 | tf_op jit(solution)/shard_map/cond/branch_4_fun/ppermute | solution.py:338
  29.0 0.0 collective-permute-done.28.refs_1_
  29.0 0.0 collective-permute-done.27.refs_0_
  29.1 5.6 %shard_map.118 = (bf16[144,1024]{1,0:T(8,128)(2,1)S(1)}, bf16[128,512]{1,0:T(8,128)(2,1)S(1)}, bf16[128,512]{1,0:T(8,128)(2,1)S(1)}, bf16[88,512]{1,0:T(8,128)(2,1)S(1)}) custom-call(s32[8]{0:T(128)S(4)} %get-tuple-element.467.flags_ref, bf16[576,512]{1,0:T(8,128)(2,1)} %get-tuple-element.477.fine_hbm, bf16[2048,1024]{1,0:T(8,128)(2,1)} %merge_hbm.1, ...), custom_call_target="tpu_custom_call" | custom-call | flops 3221225472 | bytes 12582912 | tf_op jit(solution)/shard_map/pallas_call | solution.py:274
  34.7 6.5 %conditional.5 = (bf16[2,12,24,512]{3,2,1,0:T(8,128)(2,1)}, bf16[2,6,12,1024]{3,0,2,1:T(2,128)(2,1)}) conditional(s32[]{:T(128)S(4)} %bitcast.11, (bf16[576,512]{1,0:T(8,128)(2,1)}, bf16[432,512]{1,0:T(8,128)(2,1)S(1)}, f32[32,128]{1,0:T(8,128)S(1)}, bf16[128,512]{1,0:T(8,128)(2,1)S(1)}, ...), branch_computations={%region_12.0_spmd, %region_13.0_spmd, %region_14.0_spmd, %region_1... | conditional | flops 1342177280 | bytes 6865032 | solution.py:355
  34.8 0.8 %collective-permute-start.41 = (bf16[16,512]{1,0:T(8,128)(2,1)S(1)}, bf16[16,512]{1,0:T(8,128)(2,1)S(1)}, u32[]{:S(2)}, u32[]{:S(2)}) collective-permute-start(bf16[16,512]{1,0:T(8,128)(2,1)S(1)} %slice.125), channel_id=1, source_target_pairs={{5,0},{6,1},{7,2},{4,3},{9,4},{10,5},{11,6},{8,7},{13,8},{14,9},{1... | collective-permute-start | bytes 49160 | tf_op jit(solution)/shard_map/cond/branch_1_fun/ppermute | solution.py:338
  35.6 0.7 %collective-permute-start.40 = (bf16[48,512]{1,0:T(8,128)(2,1)S(1)}, bf16[48,512]{1,0:T(8,128)(2,1)S(1)}, u32[]{:S(2)}, u32[]{:S(2)}) collective-permute-start(bf16[48,512]{1,0:T(8,128)(2,1)S(1)} %slice.124), channel_id=1, source_target_pairs={{1,0},{2,1},{3,2},{0,3},{5,4},{6,5},{7,6},{4,7},{9,8},{10,9},{11,1... | collective-permute-start | bytes 147464 | tf_op jit(solution)/shard_map/cond/branch_1_fun/ppermute | solution.py:337
  36.2 0.2 collective-permute-start.39
  36.4 2.5 %branch_1_fun.10 = bf16[2,12,24,512]{3,2,1,0:T(8,128)(2,1)} custom-call(bf16[576,512]{1,0:T(8,128)(2,1)} %get-tuple-element.393.part_hbm, bf16[432,512]{1,0:T(8,128)(2,1)S(1)} %get-tuple-element.394.source_ref, f32[32,128]{1,0:T(8,128)S(1)} %get-tuple-element.395.rows_ref.refs_3_), custom_call_target="tpu_custom_call" | custom-call | flops 1073741824 | bytes 4194304 | tf_op jit(solution)/shard_map/cond/branch_1_fun/pallas_call | solution.py:274
  38.9 0.0 collective-permute-done.41.refs_2_
  38.9 1.0 %collective-permute-done.40.refs_1_ = bf16[48,512]{1,0:T(8,128)(2,1)S(1)} collective-permute-done((bf16[48,512]{1,0:T(8,128)(2,1)S(1)}, bf16[48,512]{1,0:T(8,128)(2,1)S(1)}, u32[]{:S(2)}, u32[]{:S(2)}) %collective-permute-start.40) | collective-permute-done | bytes 49184 | tf_op jit(solution)/shard_map/cond/branch_1_fun/ppermute | solution.py:337
  39.9 0.0 collective-permute-done.39.refs_0_
  39.9 1.1 %branch_1_fun.11 = bf16[6,12,2,1024]{3,2,1,0:T(2,128)(2,1)} custom-call(bf16[144,1024]{1,0:T(8,128)(2,1)S(1)} %get-tuple-element.396.coarse_ref, bf16[48,512]{1,0:T(8,128)(2,1)S(1)} %collective-permute-done.39.refs_0_, bf16[48,512]{1,0:T(8,128)(2,1)S(1)} %collective-permute-done.40.refs_1_, bf16[16,512]{1,0:T(8,128)(2,1)S(1)} %collective-permute-done.41.refs_2_, ...), custom_call_target="tpu_custom_call" | custom-call | flops 268435456 | bytes 1048576 | tf_op jit(solution)/shard_map/cond/branch_1_fun/pallas_call | solution.py:274
  (11 shorter events, 0.1 us)
Async XLA Ops:
  2.3 9.9 %collective-permute-start.10 = (bf16[80,512]{1,0:T(8,128)(2,1)S(1)}, bf16[80,512]{1,0:T(8,128)(2,1)S(1)}, u32[]{:S(2)}, u32[]{:S(2)}) collective-permute-start(bf16[80,512]{1,0:T(8,128)(2,1)S(1)} %slice.100), channel_id=1, source_target_pairs={{1,0},{2,1},{3,2},{0,3},{5,4},{6,5},{7,6},{4,7},{9,8},{10,9},{11,1... | collective-permute-start | bytes 245768 | tf_op jit(solution)/shard_map/cond/branch_3_fun/ppermute | solution.py:337
  7.4 4.8 %collective-permute-start.9 = (bf16[80,512]{1,0:T(8,128)(2,1)S(1)}, bf16[80,512]{1,0:T(8,128)(2,1)S(1)}, u32[]{:S(2)}, u32[]{:S(2)}) collective-permute-start(bf16[80,512]{1,0:T(8,128)(2,1)S(1)} %slice.99), channel_id=1, source_target_pairs={{4,0},{8,4},{12,8},{16,12},{20,16},{24,20},{28,24},{0,28},{5,1},{9... | collective-permute-start | bytes 245768 | tf_op jit(solution)/shard_map/cond/branch_3_fun/ppermute | solution.py:339
  9.0 3.2 %collective-permute-start.11 = (bf16[16,512]{1,0:T(8,128)(2,1)S(1)}, bf16[16,512]{1,0:T(8,128)(2,1)S(1)}, u32[]{:S(2)}, u32[]{:S(2)}) collective-permute-start(bf16[16,512]{1,0:T(8,128)(2,1)S(1)} %slice.101), channel_id=1, source_target_pairs={{5,0},{6,1},{7,2},{4,3},{9,4},{10,5},{11,6},{8,7},{13,8},{14,9},{1... | collective-permute-start | bytes 49160 | tf_op jit(solution)/shard_map/cond/branch_3_fun/ppermute | solution.py:338
  18.7 10.3 %collective-permute-start.28 = (bf16[144,512]{1,0:T(8,128)(2,1)S(1)}, bf16[144,512]{1,0:T(8,128)(2,1)S(1)}, u32[]{:S(2)}, u32[]{:S(2)}) collective-permute-start(bf16[144,512]{1,0:T(8,128)(2,1)S(1)} %slice.116), channel_id=1, source_target_pairs={{3,0},{0,1},{1,2},{2,3},{7,4},{4,5},{5,6},{6,7},{11,8},{8,9},{9,10... | collective-permute-start | bytes 442376 | tf_op jit(solution)/shard_map/cond/branch_4_fun/ppermute | solution.py:337
  20.0 9.1 %collective-permute-start.27 = (bf16[144,512]{1,0:T(8,128)(2,1)S(1)}, bf16[144,512]{1,0:T(8,128)(2,1)S(1)}, u32[]{:S(2)}, u32[]{:S(2)}) collective-permute-start(bf16[144,512]{1,0:T(8,128)(2,1)S(1)} %slice.115), channel_id=1, source_target_pairs={{28,0},{0,4},{4,8},{8,12},{12,16},{16,20},{20,24},{24,28},{29,1},{... | collective-permute-start | bytes 442376 | tf_op jit(solution)/shard_map/cond/branch_4_fun/ppermute | solution.py:339
  20.0 9.0 %collective-permute-start.29 = (bf16[64,512]{1,0:T(8,128)(2,1)S(1)}, bf16[64,512]{1,0:T(8,128)(2,1)S(1)}, u32[]{:S(2)}, u32[]{:S(2)}) collective-permute-start(bf16[64,512]{1,0:T(8,128)(2,1)S(1)} %slice.117), channel_id=1, source_target_pairs={{31,0},{28,1},{29,2},{30,3},{3,4},{0,5},{1,6},{2,7},{7,8},{4,9},{5... | collective-permute-start | bytes 196616 | tf_op jit(solution)/shard_map/cond/branch_4_fun/ppermute | solution.py:338
  34.8 4.1 %collective-permute-start.41 = (bf16[16,512]{1,0:T(8,128)(2,1)S(1)}, bf16[16,512]{1,0:T(8,128)(2,1)S(1)}, u32[]{:S(2)}, u32[]{:S(2)}) collective-permute-start(bf16[16,512]{1,0:T(8,128)(2,1)S(1)} %slice.125), channel_id=1, source_target_pairs={{5,0},{6,1},{7,2},{4,3},{9,4},{10,5},{11,6},{8,7},{13,8},{14,9},{1... | collective-permute-start | bytes 49160 | tf_op jit(solution)/shard_map/cond/branch_1_fun/ppermute | solution.py:338
  35.6 4.4 %collective-permute-start.40 = (bf16[48,512]{1,0:T(8,128)(2,1)S(1)}, bf16[48,512]{1,0:T(8,128)(2,1)S(1)}, u32[]{:S(2)}, u32[]{:S(2)}) collective-permute-start(bf16[48,512]{1,0:T(8,128)(2,1)S(1)} %slice.124), channel_id=1, source_target_pairs={{1,0},{2,1},{3,2},{0,3},{5,4},{6,5},{7,6},{4,7},{9,8},{10,9},{11,1... | collective-permute-start | bytes 147464 | tf_op jit(solution)/shard_map/cond/branch_1_fun/ppermute | solution.py:337
  36.2 3.7 %collective-permute-start.39 = (bf16[48,512]{1,0:T(8,128)(2,1)S(1)}, bf16[48,512]{1,0:T(8,128)(2,1)S(1)}, u32[]{:S(2)}, u32[]{:S(2)}) collective-permute-start(bf16[48,512]{1,0:T(8,128)(2,1)S(1)} %slice.123), channel_id=1, source_target_pairs={{4,0},{8,4},{12,8},{16,12},{20,16},{24,20},{28,24},{0,28},{5,1},{9... | collective-permute-start | bytes 147464 | tf_op jit(solution)/shard_map/cond/branch_1_fun/ppermute | solution.py:339

commit v3 on v1

--- a/solution.py
+++ b/solution.py
@@ -367,7 +367,7 @@
 
     def body(shifts_hbm, tokens_hbm, table_hbm, *refs):
         outs, refs = refs[:kinds], refs[kinds:]
-        rows_ref, flags_ref, *at_refs, shifts_ref, tokens_ref, table_ref, source_ref, sems = refs
+        source_ref, rows_ref, flags_ref, *at_refs, shifts_ref, tokens_ref, table_ref, sems = refs
         start = Copies(sems)
         shift = start(shifts_hbm, shifts_ref)
         held = start(tokens_hbm, tokens_ref)
@@ -385,19 +385,18 @@
         index = columns_of(rows_of(plan, table_ref, "send_one", case), sum(plan.room_one))
         put_pieces(select_rows(index, source_ref[...]), outs)
 
-    outs = shapes(plan.room_one, width)
+    outs = shapes([*plan.room_one, count], width)
     outs += [pltpu.VMEM(plan.table.shape[1:], F32), pltpu.SMEM((8,), I32)]
     outs += [pltpu.SMEM((1,), I32)] * 3
     scratch = [pltpu.SMEM((2,), I32), pltpu.VMEM(tokens.shape, BF16), pltpu.VMEM(plan.table.shape, F32)]
-    scratch += [pltpu.VMEM((count, width), BF16)]
     got = call(body, outs, [shifts, tokens, plan.table], [HBM] * 3, scratch, 3, 1 << 28, 1 << 20)
-    sent, (rows, flags, one, two, three) = got[:kinds], got[kinds:]
-    return sent, rows, flags, one[0], two[0], three[0]
-
-
-def before_fine(flags, regions, tokens, table, weights, plan):
+    sent, (source, rows, flags, one, two, three) = got[:kinds], got[kinds:]
+    return sent, source, rows, flags, one[0], two[0], three[0]
+
+
+def before_fine(flags, regions, tokens, table, weights, plan, rows, cols):
     _, lat, lon = regions.shape
-    _, rows, cols, width = tokens.shape
+    width = tokens.shape[1]
     flat_regions = regions.reshape(2 * lat, lon)
     fine, coarse = windowed(rows, cols), natural(rows // 2, cols // 2)
 
@@ -408,13 +407,12 @@
     places = np.concatenate([lanes(fine, 1, 1), lanes(coarse, 2, 0)], axis=1)
     lines = places.shape[1]
 
-    def body(flags_ref, rows_ref, regions_hbm, places_hbm, tokens_hbm, *refs):
+    def body(flags_ref, rows_ref, tokens_ref, regions_hbm, places_hbm, *refs):
         weights_hbm, refs = refs[: len(weights)], refs[len(weights) :]
         id_ref, x_ref, *refs = refs
-        weight_refs, (regions_ref, places_ref, tokens_ref, sems) = refs[: len(weights)], refs[len(weights) :]
+        weight_refs, (regions_ref, places_ref, sems) = refs[: len(weights)], refs[len(weights) :]
         start = Copies(sems)
         waits = [start(regions_hbm, regions_ref), start(places_hbm, places_ref)]
-        held = start(tokens_hbm, tokens_ref)
         later = [start(src, dst) for src, dst in zip(weights_hbm, weight_refs)]
         for copy in waits:
             copy.wait()
@@ -440,18 +438,17 @@
         ids = jnp.sum(jnp.where(line == along(col), picked, 0.0), axis=0, keepdims=True) + along(wrapped)
         for n in range(lines):
             id_ref[n : n + 1, :] = ids[:, n * 128 : (n + 1) * 128]
-        held.wait()
         take = columns_of(rows_of(plan, rows_ref, "take_one"), len(fine))
-        x_ref[...] = select_rows(take, flat(tokens_ref)).astype(BF16)
+        x_ref[...] = select_rows(take, tokens_ref[...]).astype(BF16)
         for copy in later:
             copy.wait()
 
     outs = [pltpu.VMEM((lines, 128), F32)] + shapes([len(fine)], width)
     outs += [pltpu.VMEM(w.shape, BF16) for w in weights]
-    scratch = [pltpu.VMEM(flat_regions.shape, I32), pltpu.VMEM(places.shape, F32), pltpu.VMEM(tokens.shape, BF16)]
-    args = [flags, table, flat_regions, places, tokens, *weights]
-    in_specs = [SMEM, VMEM] + [HBM] * (3 + len(weights))
-    ids, x, *weights = call(body, outs, args, in_specs, scratch, 3 + len(weights), 1 << 28, 4 << 20)
+    scratch = [pltpu.VMEM(flat_regions.shape, I32), pltpu.VMEM(places.shape, F32)]
+    args = [flags, table, tokens, flat_regions, places, *weights]
+    in_specs = [SMEM, VMEM, VMEM] + [HBM] * (2 + len(weights))
+    ids, x, *weights = call(body, outs, args, in_specs, scratch, 2 + len(weights), 1 << 28, 4 << 20)
     return ids, x, weights
 
 
@@ -460,37 +457,46 @@
     return jnp.where(columns_of(lines, count) == lane, 1.0, 0.0).astype(BF16)
 
 
-def before_coarse(fine, table, weight, plan):
+def before_coarse(flags, fine, table, weight, plan):
     own, width = fine.shape
     half = 3 * weight.shape[0] // 8
 
-    def body(rows_ref, fine_hbm, weight_hbm, x_ref, part_hbm, weight_ref, fine_ref, part_ref, sems):
+    def body(flags_ref, rows_ref, fine_ref, weight_hbm, x_ref, part_hbm, home_ref, weight_ref, part_ref, sems):
         start = Copies(sems)
-        held = start(fine_hbm, fine_ref)
         later = start(weight_hbm.at[pl.ds(0, half)], weight_ref)
         take = columns_of(rows_of(plan, rows_ref, "fine_out"), own)
-        held.wait()
         part_ref[...] = select_rows(take, fine_ref[...]).astype(BF16)
         leave = start(part_ref, part_hbm)
         take = columns_of(rows_of(plan, rows_ref, "take_two"), own)
         x_ref[...] = select_rows(take, fine_ref[...]).astype(BF16)
+
+        @pl.when(needs_fine(flags_ref, plan))
+        def _():
+            index = columns_of(rows_of(plan, rows_ref, "send_four"), sum(plan.room_four))
+            home_ref[...] = select_rows(index, fine_ref[...]).astype(BF16)
+
         leave.wait()
         later.wait()
 
-    outs = shapes([own], width) + shapes([own], width, pltpu.HBM) + shapes([half], weight.shape[1])
-    scratch = [pltpu.VMEM(fine.shape, BF16)] * 2
-    return call(body, outs, [table, fine, weight], [VMEM, HBM, HBM], scratch, 3, 1 << 28, 4 << 20)
+    outs = shapes([own], width) + shapes([own], width, pltpu.HBM)
+    outs += shapes([sum(plan.room_four)], width) + shapes([half], weight.shape[1])
+    scratch = [pltpu.VMEM(fine.shape, BF16)]
+    args = [flags, table, fine, weight]
+    return call(body, outs, args, [SMEM, VMEM, VMEM, HBM], scratch, 2, 1 << 28, 4 << 20)
+
+
+def needs_fine(flags_ref, plan):
+    with_fine = [n for n, sizes in enumerate(plan.four) if sum(sizes)]
+    return functools.reduce(jnp.logical_or, [flags_ref[0] == n for n in with_fine])
 
 
 def fine_level(x_own, source, ids, w_qkv, w_proj, rows, plan):
     count, width = x_own.shape
     inner = w_proj.shape[0]
 
-    def body(own_ref, source_ref, ids_ref, qkv_w_ref, proj_w_ref, rows_ref, out_hbm, *refs):
-        *piece_outs, x_ref, qkv_ref, out_ref, id_ref, sems = refs
-        start = Copies(sems)
+    def body(own_ref, source_ref, ids_ref, qkv_w_ref, proj_w_ref, rows_ref, out_ref, *refs):
+        *piece_outs, x_ref, qkv_ref, id_ref, _ = refs
         id_ref[...] = id_columns(ids_ref[: -(-count // 128), :], count)
-        leave = []
         take = columns_of(rows_of(plan, rows_ref, "take_one"), count) - float(count)
         x = own_ref[...].astype(F32) + select_rows(take, source_ref[...])
         x_ref[...] = x
@@ -501,7 +507,6 @@
             at = slice(w * TOK, (w + 1) * TOK)
             out = jnp.dot(out, proj_w_ref[...], preferred_element_type=F32)
             out_ref[at, :] = (x_ref[at, :] + out).astype(BF16)
-            leave.append(start(out_ref.at[pl.ds(w * TOK, TOK)], out_hbm.at[pl.ds(w * TOK, TOK)]))
 
         attend_windows(
             lambda w, at: qkv_ref[w * TOK : (w + 1) * TOK, at : at + 128],
@@ -512,36 +517,30 @@
         )
         index = columns_of(rows_of(plan, rows_ref, "send_two"), sum(plan.room_two))
         put_pieces(select_rows(index, out_ref[...]), piece_outs)
-        for copy in leave:
-            copy.wait()
-
-    outs = shapes([count], width, pltpu.HBM) + shapes(plan.room_two, width)
+
+    outs = shapes([count, *plan.room_two], width)
     scratch = [
         pltpu.VMEM((count, width), F32),
         pltpu.VMEM((count, 3 * inner), BF16),
-        pltpu.VMEM((count, width), BF16),
         pltpu.VMEM((count, 128), BF16),
     ]
     args = [x_own, source, ids, w_qkv, w_proj, rows]
-    out, *sent = call(body, outs, args, [VMEM] * len(args), scratch, count // TOK, 3 << 30, 6 << 20, 14)
+    out, *sent = call(body, outs, args, [VMEM] * len(args), scratch, 1, 3 << 30, 6 << 20, 14)
     return out, sent
 
 
-def coarse_level(flags, fine, x_own, source, ids, merge_first, w_merge, w_qkv, w_proj, rows, plan):
+def coarse_level(flags, home, x_own, source, ids, merge_first, w_merge, w_qkv, w_proj, rows, plan):
     depth, width = w_merge.shape
-    own, half = fine.shape
+    own, half = x_own.shape
     count = own // 4
     inner = w_proj.shape[0]
 
     def body(
-        flags_ref, fine_hbm, merge_hbm, qkv_w_hbm, proj_w_hbm, own_ref, source_ref, ids_ref, first_ref, rows_ref, *refs
+        flags_ref, merge_hbm, qkv_w_hbm, proj_w_hbm, home_ref, own_ref, source_ref, ids_ref, first_ref, rows_ref, *refs
     ):
         out_ref, *piece_outs = refs[:4]
-        qkv_ref, fine_ref, id_ref, merge_ref, qkv_w_ref, proj_w_ref, sems = refs[4:]
+        qkv_ref, id_ref, merge_ref, qkv_w_ref, proj_w_ref, sems = refs[4:]
         start = Copies(sems)
-        with_fine = [n for n, sizes in enumerate(plan.four) if sum(sizes)]
-        needs_fine = functools.reduce(jnp.logical_or, [flags_ref[0] == n for n in with_fine])
-
         def bring(src, dst):
             cuts = [(at, min(half, src.shape[0] - at)) for at in range(0, src.shape[0], half)]
             return [(at, size, start(src.at[pl.ds(at, size)], dst.at[pl.ds(at, size)])) for at, size in cuts]
@@ -557,12 +556,6 @@
         merge_w = bring(merge_hbm.at[pl.ds(here, depth - here)], merge_ref)
         qkv_w = bring(qkv_w_hbm, qkv_w_ref)
         proj_w = start(proj_w_hbm, proj_w_ref)
-        fine_copy = (fine_hbm, fine_ref, sems.at[start.used])
-
-        @pl.when(needs_fine)
-        def _():
-            pltpu.make_async_copy(*fine_copy).start()
-
         id_ref[...] = id_columns(ids_ref[-(-own // 128) :, :], count)
         take = columns_of(rows_of(plan, rows_ref, "take_two"), 4 * count) - float(own)
         x = own_ref[...].astype(F32) + select_rows(take, source_ref[...])
@@ -591,27 +584,23 @@
                     ref[size : 2 * size, :] = sent[at : at + size, half:]
                     at += space
 
-        @pl.when(needs_fine)
-        def _():
-            pltpu.make_async_copy(*fine_copy).wait()
-            index = columns_of(rows_of(plan, rows_ref, "send_four"), sum(plan.room_four))
-            sent = select_rows(index, fine_ref[...]).astype(BF16)
-            for n in with_fine:
+        for n, fine_sizes in enumerate(plan.four):
+            if sum(fine_sizes):
 
                 @pl.when(flags_ref[0] == n)
                 def _():
                     at = 0
-                    for ref, size, more, space in zip(piece_outs, plan.three[n], plan.four[n], plan.room_four):
-                        ref[2 * size : 2 * size + more, :] = sent[at : at + more]
+                    for ref, size, more, space in zip(piece_outs, plan.three[n], fine_sizes, plan.room_four):
+                        ref[2 * size : 2 * size + more, :] = home_ref[at : at + more, :]
                         at += space
 
     most = [max(2 * three[k] + four[k] for three, four in zip(plan.three, plan.four)) for k in range(3)]
     outs = shapes([count], width) + shapes(most, half)
     scratch = [pltpu.VMEM((count, 3 * inner), BF16)]
-    shapes_in = [fine.shape, (count, 128), (depth - merge_first.shape[0], width), w_qkv.shape, w_proj.shape]
+    shapes_in = [(count, 128), (depth - merge_first.shape[0], width), w_qkv.shape, w_proj.shape]
     scratch += [pltpu.VMEM(shape, BF16) for shape in shapes_in]
-    args = [flags, fine, w_merge, w_qkv, w_proj, x_own, source, ids, merge_first, rows]
-    in_specs = [SMEM] + [HBM] * 4 + [VMEM] * (len(args) - 5)
+    args = [flags, w_merge, w_qkv, w_proj, home, x_own, source, ids, merge_first, rows]
+    in_specs = [SMEM] + [HBM] * 3 + [VMEM] * (len(args) - 4)
     copies = depth // half + width // half + 3
     out, *sent = call(body, outs, args, in_specs, scratch, copies, 3 << 30, 12 << 20, 24)
     return out, sent
@@ -690,7 +679,7 @@
 
     def first(which, sign, sent, *args):
         got = exchange(sent, plan.one[which], sign)
-        return lay(got, plan.room_one), before_fine(*args, plan)
+        return lay(got, plan.room_one), before_fine(*args, plan, rows, cols)
 
     def second(which, sign, sent, *args):
         got = exchange(sent, plan.two[which], sign)
@@ -711,14 +700,16 @@
     def branches(stage, pairs):
         return [functools.partial(stage, which, sign) for which, sign in pairs]
 
-    sent, table, flags, one, two, three = first_pieces(shifts, tokens, plan)
+    sent, source, table, flags, one, two, three = first_pieces(shifts, tokens, plan)
     got, (ids, x, weights) = choose(
-        one, branches(first, plan.one_branches), sent, flags, regions, tokens, table, [fine_qkv, fine_proj]
+        one, branches(first, plan.one_branches), sent, flags, regions, source, table, [fine_qkv, fine_proj]
     )
     fine, sent = fine_level(x, got, ids, *weights, table, plan)
-    got, (x, part, merge_first) = choose(two, branches(second, plan.two_branches), sent, fine, table, merge_weight)
+    got, (x, part, home, merge_first) = choose(
+        two, branches(second, plan.two_branches), sent, flags, fine, table, merge_weight
+    )
     coarse, sent = coarse_level(
-        flags, fine, x, got, ids, merge_first, merge_weight, coarse_qkv, coarse_proj, table, plan
+        flags, home, x, got, ids, merge_first, merge_weight, coarse_qkv, coarse_proj, table, plan
     )
     return choose(three, branches(third, plan.three_branches), sent, part, got, coarse, table)
 

time: 41.2 us -> 42 us (1.019); the launches traced: 41 us -> 42.5 us
  local copies, waits for them, and re-layouts: 0.04 us -> 2.92 us
  starting transfers between devices: 13.9 us -> 11.3 us
  waiting for transfers between devices: 5.24 us -> 7.76 us
  Pallas kernels: 20.3 us -> 19 us
    ppermute x3, waiting for transfers between devices: 3.99 us -> 6.39 us  [exchange(): both = lax.ppermute(both, ('lat', 'lon'), pairs)]
    ppermute x3, starting transfers between devices: 8.22 us -> 5.87 us  [exchange(): both = lax.ppermute(both, ('lat', 'lon'), pairs)]
    unnamed x0 -> x4, local copies, waits for them, and re-layouts: none -> 2.1 us
    pallas_call x9, Pallas kernels: 20.3 us -> 19 us  [call(): pl.pallas_call(body, out_shape=outs, in_specs=in_specs, out_specs=out_spe...]
    cond x0 -> x4, local copies, waits for them, and re-layouts: none -> 0.79 us
  transfers between devices with their start and end apart: 9 -> 9, of which waited for: 2 -> 5; matrix products, arithmetic and copies ran while one was open for 0% -> 0% of each run, Pallas kernels for 17% -> 13%
where the time goes in v3:
time: 42 us; the launch traced here: 42.5 us
  Pallas kernels  19 us (45%)
  starting transfers between devices  11.3 us (27%)
  waiting for transfers between devices  7.76 us (18%)
  local copies, waits for them, and re-layouts  2.92 us (7%)
  between operations  0.87 us (2%)
  loops' own time  0.62 us (1%)
    pallas_call x9, Pallas kernels, call(): pl.pallas_call(body, out_shape=outs, in_specs=in_specs, out_specs=out_spe...  19 us
    ppermute x3, waiting for transfers between devices, exchange(): both = lax.ppermute(both, ('lat', 'lon'), pairs)  6.39 us
    ppermute x3, starting transfers between devices, exchange(): both = lax.ppermute(both, ('lat', 'lon'), pairs)  5.87 us
    ppermute x3, starting transfers between devices, exchange(): col = lax.ppermute(col, 'lon', [((j + sign) % lon, j) for j in range(lon)])  4.26 us
    unnamed x4, local copies, waits for them, and re-layouts  2.1 us
    ppermute x3, waiting for transfers between devices, exchange(): col = lax.ppermute(col, 'lon', [((j + sign) % lon, j) for j in range(lon)])  1.36 us
    ppermute x3, starting transfers between devices, exchange(): row = lax.ppermute(row, 'lat', [((i + sign) % lat, i) for i in range(lat)])  1.13 us
  transfers between devices with their start and end apart: 9, of which 5 were waited for; matrix products, arithmetic and copies ran while one was open for 0% of the time, Pallas kernels for 13%

profile of v3, /device:TPU:0, one launch (start us, length us, event | category | flops | bytes accessed | tf_op | source)
XLA Modules:
  0.0 42.5 jit_solution(6450402977315489943)
XLA Ops:
  0.6 1.6 %shard_map.116 = (bf16[112,512]{1,0:T(8,128)(2,1)S(1)}, bf16[112,512]{1,0:T(8,128)(2,1)S(1)}, bf16[48,512]{1,0:T(8,128)(2,1)S(1)}, bf16[576,512]{1,0:T(8,128)(2,...) custom-call(s32[2]{0:T(128)} %shifts_hbm.1, ...), custom_call_target="tpu_custom_call" | custom-call | flops 268435456 | bytes 1048576 | tf_op jit(solution)/shard_map/pallas_call | solution.py:275
  2.2 9.9 %conditional.3 = (bf16[272,512]{1,0:T(8,128)(2,1)S(1)}, f32[7,128]{1,0:T(8,128)S(1)}, bf16[576,512]{1,0:T(8,128)(2,1)S(1)}, bf16[512,1536]{1,0:T(8,128)(2,1)S(1)}, bf16[512,512]{1,0:T(8,128)(2,1)}) conditional(s32[]{:T(128)S(4)} %bitcast.13, (bf16[112,512]{1,0:T(8,128)(2,1)S(1)}, bf16[112,512]{1,0:T(8,128)(2,1)S(1)}, ...), branch_computations={%region_0.0_spmd, %region_1.0_spmd, %region_2.0_spmd, %region_3.0_... | conditional | flops 268435456 | bytes 7717052 | solution.py:356
  2.2 3.1 %collective-permute-start.1 = (bf16[48,512]{1,0:T(8,128)(2,1)S(1)}, bf16[48,512]{1,0:T(8,128)(2,1)S(1)}, u32[]{:S(2)}, u32[]{:S(2)}) collective-permute-start(bf16[48,512]{1,0:T(8,128)(2,1)S(1)} %slice.91), channel_id=1, source_target_pairs={{3,0},{0,1},{1,2},{2,3},{7,4},{4,5},{5,6},{6,7},{11,8},{8,9},{9,10... | collective-permute-start | bytes 147464 | tf_op jit(solution)/shard_map/cond/branch_0_fun/ppermute | solution.py:338
  5.3 0.0 collective-permute-start
  5.3 2.8 %collective-permute-start.2 = (bf16[8,512]{1,0:T(8,128)(2,1)S(1)}, bf16[8,512]{1,0:T(8,128)(2,1)S(1)}, u32[]{:S(2)}, u32[]{:S(2)}) collective-permute-start(bf16[8,512]{1,0:T(8,128)(2,1)S(1)} %slice.92), channel_id=1, source_target_pairs={{31,0},{28,1},{29,2},{30,3},{3,4},{0,5},{1,6},{2,7},{7,8},{4,9},{5... | collective-permute-start | bytes 24584 | tf_op jit(solution)/shard_map/cond/branch_0_fun/ppermute | solution.py:339
  8.1 1.7 %branch_0_fun.7 = (f32[7,128]{1,0:T(8,128)S(1)}, bf16[576,512]{1,0:T(8,128)(2,1)S(1)}, bf16[512,1536]{1,0:T(8,128)(2,1)S(1)}, bf16[512,512]{1,0:T(8,128)(2,1)S(1)}) custom-call(s32[8]{0:T(128)S(4)} %get-tuple-element.275.flags_ref, f32[32,128]{1,0:T(8,128)S(1)} %get-tuple-element.276.rows_ref, bf16[576,512]{1,0:T(8,128)(2,1)S(1)} %get-tuple-element.277.tokens_ref, ...), custom_call_target="tpu_custom_call" | custom-call | flops 268435456 | bytes 4194304 | tf_op jit(solution)/shard_map/cond/branch_0_fun/pallas_call | solution.py:275
  9.8 0.0 copy-start.8
  9.8 0.8 %copy-done.8 = bf16[512,512]{1,0:T(8,128)(2,1)} copy-done((bf16[512,512]{1,0:T(8,128)(2,1)}, bf16[512,512]{1,0:T(8,128)(2,1)S(1)}, u32[]{:S(2)}) %copy-start.8) | copy-done | bytes 524312 | tf_op jit(solution)/shard_map/cond
  10.6 1.4 %collective-permute-done.2.refs_2_ = bf16[8,512]{1,0:T(8,128)(2,1)S(1)} collective-permute-done((bf16[8,512]{1,0:T(8,128)(2,1)S(1)}, bf16[8,512]{1,0:T(8,128)(2,1)S(1)}, u32[]{:S(2)}, u32[]{:S(2)}) %collective-permute-start.2) | collective-permute-done | bytes 8224 | tf_op jit(solution)/shard_map/cond/branch_0_fun/ppermute | solution.py:339
  12.1 0.0 collective-permute-done.1.refs_1_
  12.1 0.0 collective-permute-done.refs_0_
  12.1 0.0 copy-start.13
  12.1 1.0 %copy-done.13 = bf16[512,512]{1,0:T(8,128)(2,1)S(1)} copy-done((bf16[512,512]{1,0:T(8,128)(2,1)S(1)}, bf16[512,512]{1,0:T(8,128)(2,1)}, u32[]{:S(2)}) %copy-start.13) | copy-done | bytes 524312
  13.2 5.6 %shard_map.117 = (bf16[576,512]{1,0:T(8,128)(2,1)S(1)}, bf16[160,512]{1,0:T(8,128)(2,1)S(1)}, bf16[160,512]{1,0:T(8,128)(2,1)S(1)}, bf16[112,512]{1,0:T(8,128)(2,1)S(1)}) custom-call(bf16[576,512]{1,0:T(8,128)(2,1)S(1)} %get-tuple-element.500.own_ref, bf16[272,512]{1,0:T(8,128)(2,1)S(1)} %get-tuple-element.501.source_ref, ...), custom_call_target="tpu_custom_call" | custom-call | flops 3221225472 | bytes 6291456 | tf_op jit(solution)/shard_map/pallas_call | solution.py:275
  18.8 8.1 %conditional.4 = (bf16[432,512]{1,0:T(8,128)(2,1)S(1)}, bf16[576,512]{1,0:T(8,128)(2,1)}, bf16[576,512]{1,0:T(8,128)(2,1)}, bf16[112,512]{1,0:T(8,128)(2,1)S(1)}, bf16[768,1024]{1,0:T(8,128)(2,1)S(1)}) conditional(s32[]{:T(128)S(4)} %bitcast.12, (bf16[160,512]{1,0:T(8,128)(2,1)S(1)}, bf16[160,512]{1,0:T(8,128)(2,1)S(1)}, ...), branch_computations={%region_5.0_spmd, %region_6.0_spmd, %region_7.0_spmd, %region_8.0_... | conditional | flops 268435456 | bytes 8978620 | solution.py:356
  19.0 1.1 %collective-permute-start.33 = (bf16[160,512]{1,0:T(8,128)(2,1)S(1)}, bf16[160,512]{1,0:T(8,128)(2,1)S(1)}, u32[]{:S(2)}, u32[]{:S(2)}) collective-permute-start(bf16[160,512]{1,0:T(8,128)(2,1)S(1)} %get-tuple-element.403), channel_id=1, source_target_pairs={{4,0},{8,4},{12,8},{16,12},{20,16},{24,20},{28,24},{0,28},{5,1},{9... | collective-permute-start | bytes 491528 | tf_op jit(solution)/shard_map/cond/branch_6_fun/ppermute | solution.py:340
  20.2 0.7 %collective-permute-start.34 = (bf16[160,512]{1,0:T(8,128)(2,1)S(1)}, bf16[160,512]{1,0:T(8,128)(2,1)S(1)}, u32[]{:S(2)}, u32[]{:S(2)}) collective-permute-start(bf16[160,512]{1,0:T(8,128)(2,1)S(1)} %get-tuple-element.404), channel_id=1, source_target_pairs={{1,0},{2,1},{3,2},{0,3},{5,4},{6,5},{7,6},{4,7},{9,8},{10,9},{11,1... | collective-permute-start | bytes 491528 | tf_op jit(solution)/shard_map/cond/branch_6_fun/ppermute | solution.py:338
  20.8 1.4 %collective-permute-start.35 = (bf16[104,512]{1,0:T(8,128)(2,1)S(1)}, bf16[104,512]{1,0:T(8,128)(2,1)S(1)}, u32[]{:S(2)}, u32[]{:S(2)}) collective-permute-start(bf16[104,512]{1,0:T(8,128)(2,1)S(1)} %slice.119), channel_id=1, source_target_pairs={{5,0},{6,1},{7,2},{4,3},{9,4},{10,5},{11,6},{8,7},{13,8},{14,9},{1... | collective-permute-start | bytes 319496 | tf_op jit(solution)/shard_map/cond/branch_6_fun/ppermute | solution.py:339
  22.2 1.5 %branch_6_fun.3 = (bf16[576,512]{1,0:T(8,128)(2,1)S(1)}, bf16[576,512]{1,0:T(8,128)(2,1)}, bf16[112,512]{1,0:T(8,128)(2,1)S(1)}, bf16[768,1024]{1,0:T(8,128)(2,1)S(1)}) custom-call(s32[8]{0:T(128)S(4)} %get-tuple-element.406.flags_ref, f32[32,128]{1,0:T(8,128)S(1)} %get-tuple-element.407.rows_ref, bf16[576,512]{1,0:T(8,128)(2,1)S(1)} %get-tuple-element.408.fine_ref, ...), custom_call_target="tpu_custom_call" | custom-call | flops 268435456 | bytes 4194304 | tf_op jit(solution)/shard_map/cond/branch_6_fun/pallas_call | solution.py:275
  23.8 0.0 copy-start.6
  23.8 2.6 %collective-permute-done.35.refs_2_ = bf16[104,512]{1,0:T(8,128)(2,1)S(1)} collective-permute-done((bf16[104,512]{1,0:T(8,128)(2,1)S(1)}, bf16[104,512]{1,0:T(8,128)(2,1)S(1)}, u32[]{:S(2)}, u32[]{:S(2)}) %collective-permute-start.35) | collective-permute-done | bytes 106528 | tf_op jit(solution)/shard_map/cond/branch_6_fun/ppermute | solution.py:339
  26.4 0.0 collective-permute-done.33.refs_0_
  26.4 0.5 %collective-permute-done.34.refs_1_ = bf16[160,512]{1,0:T(8,128)(2,1)S(1)} collective-permute-done((bf16[160,512]{1,0:T(8,128)(2,1)S(1)}, bf16[160,512]{1,0:T(8,128)(2,1)S(1)}, u32[]{:S(2)}, u32[]{:S(2)}) %collective-permute-start.34) | collective-permute-done | bytes 163872 | tf_op jit(solution)/shard_map/cond/branch_6_fun/ppermute | solution.py:338
  26.9 0.0 copy-done.6
  26.9 0.0 copy-start.7
  26.9 1.1 %copy-done.7 = bf16[576,512]{1,0:T(8,128)(2,1)S(1)} copy-done((bf16[576,512]{1,0:T(8,128)(2,1)S(1)}, bf16[576,512]{1,0:T(8,128)(2,1)}, u32[]{:S(2)}) %copy-start.7) | copy-done | bytes 589848
  28.0 5.0 %shard_map.118 = (bf16[144,1024]{1,0:T(8,128)(2,1)S(1)}, bf16[128,512]{1,0:T(8,128)(2,1)S(1)}, bf16[128,512]{1,0:T(8,128)(2,1)S(1)}, bf16[88,512]{1,0:T(8,128)(2,1)S(1)}) custom-call(s32[8]{0:T(128)S(4)} %get-tuple-element.497.flags_ref, bf16[2048,1024]{1,0:T(8,128)(2,1)} %merge_hbm.1, bf16[1024,1536]{1,0:T(8,128)(2,1)} %qkv_w_hbm.1, ...), custom_call_target="tpu_custom_call" | custom-call | flops 3221225472 | bytes 12582912 | tf_op jit(solution)/shard_map/pallas_call | solution.py:275
  32.9 9.4 %conditional.5 = (bf16[2,12,24,512]{3,2,1,0:T(8,128)(2,1)}, bf16[2,6,12,1024]{3,0,2,1:T(2,128)(2,1)}) conditional(s32[]{:T(128)S(4)} %bitcast.11, (bf16[576,512]{1,0:T(8,128)(2,1)}, bf16[432,512]{1,0:T(8,128)(2,1)S(1)}, f32[32,128]{1,0:T(8,128)S(1)}, bf16[128,512]{1,0:T(8,128)(2,1)S(1)}, ...), branch_computations={%region_12.0_spmd, %region_13.0_spmd, %region_14.0_spmd, %region_1... | conditional | flops 1342177280 | bytes 6865032 | solution.py:356
  33.0 1.7 %collective-permute-start.44 = (bf16[32,512]{1,0:T(8,128)(2,1)S(1)}, bf16[32,512]{1,0:T(8,128)(2,1)S(1)}, u32[]{:S(2)}, u32[]{:S(2)}) collective-permute-start(bf16[32,512]{1,0:T(8,128)(2,1)S(1)} %slice.128), channel_id=1, source_target_pairs={{31,0},{28,1},{29,2},{30,3},{3,4},{0,5},{1,6},{2,7},{7,8},{4,9},{5... | collective-permute-start | bytes 98312 | tf_op jit(solution)/shard_map/cond/branch_2_fun/ppermute | solution.py:339
  34.7 0.5 %collective-permute-start.43 = (bf16[64,512]{1,0:T(8,128)(2,1)S(1)}, bf16[64,512]{1,0:T(8,128)(2,1)S(1)}, u32[]{:S(2)}, u32[]{:S(2)}) collective-permute-start(bf16[64,512]{1,0:T(8,128)(2,1)S(1)} %slice.127), channel_id=1, source_target_pairs={{3,0},{0,1},{1,2},{2,3},{7,4},{4,5},{5,6},{6,7},{11,8},{8,9},{9,10... | collective-permute-start | bytes 196616 | tf_op jit(solution)/shard_map/cond/branch_2_fun/ppermute | solution.py:338
  35.2 0.0 collective-permute-start.42
  35.2 2.5 %branch_2_fun.10 = bf16[2,12,24,512]{3,2,1,0:T(8,128)(2,1)} custom-call(bf16[576,512]{1,0:T(8,128)(2,1)} %get-tuple-element.428.part_hbm, bf16[432,512]{1,0:T(8,128)(2,1)S(1)} %get-tuple-element.429.source_ref, f32[32,128]{1,0:T(8,128)S(1)} %get-tuple-element.430.rows_ref.refs_3_), custom_call_target="tpu_custom_call" | custom-call | flops 1073741824 | bytes 4194304 | tf_op jit(solution)/shard_map/cond/branch_2_fun/pallas_call | solution.py:275
  37.7 2.4 %collective-permute-done.44.refs_2_ = bf16[32,512]{1,0:T(8,128)(2,1)S(1)} collective-permute-done((bf16[32,512]{1,0:T(8,128)(2,1)S(1)}, bf16[32,512]{1,0:T(8,128)(2,1)S(1)}, u32[]{:S(2)}, u32[]{:S(2)}) %collective-permute-start.44) | collective-permute-done | bytes 32800 | tf_op jit(solution)/shard_map/cond/branch_2_fun/ppermute | solution.py:339
  40.1 0.9 %collective-permute-done.43.refs_1_ = bf16[64,512]{1,0:T(8,128)(2,1)S(1)} collective-permute-done((bf16[64,512]{1,0:T(8,128)(2,1)S(1)}, bf16[64,512]{1,0:T(8,128)(2,1)S(1)}, u32[]{:S(2)}, u32[]{:S(2)}) %collective-permute-start.43) | collective-permute-done | bytes 65568 | tf_op jit(solution)/shard_map/cond/branch_2_fun/ppermute | solution.py:338
  41.0 0.0 collective-permute-done.42.refs_0_
  41.0 1.1 %branch_2_fun.11 = bf16[6,12,2,1024]{3,2,1,0:T(2,128)(2,1)} custom-call(bf16[144,1024]{1,0:T(8,128)(2,1)S(1)} %get-tuple-element.431.coarse_ref, bf16[64,512]{1,0:T(8,128)(2,1)S(1)} %collective-permute-done.42.refs_0_, bf16[64,512]{1,0:T(8,128)(2,1)S(1)} %collective-permute-done.43.refs_1_, bf16[32,512]{1,0:T(8,128)(2,1)S(1)} %collective-permute-done.44.refs_2_, ...), custom_call_target="tpu_custom_call" | custom-call | flops 268435456 | bytes 1048576 | tf_op jit(solution)/shard_map/cond/branch_2_fun/pallas_call | solution.py:275
  (9 shorter events, 0.1 us)
Async XLA Ops:
  2.2 9.8 %collective-permute-start.1 = (bf16[48,512]{1,0:T(8,128)(2,1)S(1)}, bf16[48,512]{1,0:T(8,128)(2,1)S(1)}, u32[]{:S(2)}, u32[]{:S(2)}) collective-permute-start(bf16[48,512]{1,0:T(8,128)(2,1)S(1)} %slice.91), channel_id=1, source_target_pairs={{3,0},{0,1},{1,2},{2,3},{7,4},{4,5},{5,6},{6,7},{11,8},{8,9},{9,10... | collective-permute-start | bytes 147464 | tf_op jit(solution)/shard_map/cond/branch_0_fun/ppermute | solution.py:338
  5.3 6.7 %collective-permute-start = (bf16[48,512]{1,0:T(8,128)(2,1)S(1)}, bf16[48,512]{1,0:T(8,128)(2,1)S(1)}, u32[]{:S(2)}, u32[]{:S(2)}) collective-permute-start(bf16[48,512]{1,0:T(8,128)(2,1)S(1)} %slice.90), channel_id=1, source_target_pairs={{28,0},{0,4},{4,8},{8,12},{12,16},{16,20},{20,24},{24,28},{29,1},{... | collective-permute-start | bytes 147464 | tf_op jit(solution)/shard_map/cond/branch_0_fun/ppermute | solution.py:340
  5.3 6.7 %collective-permute-start.2 = (bf16[8,512]{1,0:T(8,128)(2,1)S(1)}, bf16[8,512]{1,0:T(8,128)(2,1)S(1)}, u32[]{:S(2)}, u32[]{:S(2)}) collective-permute-start(bf16[8,512]{1,0:T(8,128)(2,1)S(1)} %slice.92), channel_id=1, source_target_pairs={{31,0},{28,1},{29,2},{30,3},{3,4},{0,5},{1,6},{2,7},{7,8},{4,9},{5... | collective-permute-start | bytes 24584 | tf_op jit(solution)/shard_map/cond/branch_0_fun/ppermute | solution.py:339
  9.8 0.8 %copy-start.8 = (bf16[512,512]{1,0:T(8,128)(2,1)}, bf16[512,512]{1,0:T(8,128)(2,1)S(1)}, u32[]{:S(2)}) copy-start(bf16[512,512]{1,0:T(8,128)(2,1)S(1)} %get-tuple-element.524) | copy-start | bytes 1572868 | tf_op jit(solution)/shard_map/cond
  12.1 1.0 %copy-start.13 = (bf16[512,512]{1,0:T(8,128)(2,1)S(1)}, bf16[512,512]{1,0:T(8,128)(2,1)}, u32[]{:S(2)}) copy-start(bf16[512,512]{1,0:T(8,128)(2,1)} %get-tuple-element.504.proj_w_ref) | copy-start | bytes 1572868
  19.0 7.3 %collective-permute-start.33 = (bf16[160,512]{1,0:T(8,128)(2,1)S(1)}, bf16[160,512]{1,0:T(8,128)(2,1)S(1)}, u32[]{:S(2)}, u32[]{:S(2)}) collective-permute-start(bf16[160,512]{1,0:T(8,128)(2,1)S(1)} %get-tuple-element.403), channel_id=1, source_target_pairs={{4,0},{8,4},{12,8},{16,12},{20,16},{24,20},{28,24},{0,28},{5,1},{9... | collective-permute-start | bytes 491528 | tf_op jit(solution)/shard_map/cond/branch_6_fun/ppermute | solution.py:340
  20.2 6.7 %collective-permute-start.34 = (bf16[160,512]{1,0:T(8,128)(2,1)S(1)}, bf16[160,512]{1,0:T(8,128)(2,1)S(1)}, u32[]{:S(2)}, u32[]{:S(2)}) collective-permute-start(bf16[160,512]{1,0:T(8,128)(2,1)S(1)} %get-tuple-element.404), channel_id=1, source_target_pairs={{1,0},{2,1},{3,2},{0,3},{5,4},{6,5},{7,6},{4,7},{9,8},{10,9},{11,1... | collective-permute-start | bytes 491528 | tf_op jit(solution)/shard_map/cond/branch_6_fun/ppermute | solution.py:338
  20.8 5.5 %collective-permute-start.35 = (bf16[104,512]{1,0:T(8,128)(2,1)S(1)}, bf16[104,512]{1,0:T(8,128)(2,1)S(1)}, u32[]{:S(2)}, u32[]{:S(2)}) collective-permute-start(bf16[104,512]{1,0:T(8,128)(2,1)S(1)} %slice.119), channel_id=1, source_target_pairs={{5,0},{6,1},{7,2},{4,3},{9,4},{10,5},{11,6},{8,7},{13,8},{14,9},{1... | collective-permute-start | bytes 319496 | tf_op jit(solution)/shard_map/cond/branch_6_fun/ppermute | solution.py:339
  23.8 3.1 %copy-start.6 = (bf16[576,512]{1,0:T(8,128)(2,1)}, bf16[576,512]{1,0:T(8,128)(2,1)S(1)}, u32[]{:S(2)}) copy-start(bf16[576,512]{1,0:T(8,128)(2,1)S(1)} %get-tuple-element.576) | copy-start | bytes 1769476 | tf_op jit(solution)/shard_map/cond
  26.9 1.1 %copy-start.7 = (bf16[576,512]{1,0:T(8,128)(2,1)S(1)}, bf16[576,512]{1,0:T(8,128)(2,1)}, u32[]{:S(2)}) copy-start(bf16[576,512]{1,0:T(8,128)(2,1)} %get-tuple-element.512.own_ref) | copy-start | bytes 1769476
  33.0 7.1 %collective-permute-start.44 = (bf16[32,512]{1,0:T(8,128)(2,1)S(1)}, bf16[32,512]{1,0:T(8,128)(2,1)S(1)}, u32[]{:S(2)}, u32[]{:S(2)}) collective-permute-start(bf16[32,512]{1,0:T(8,128)(2,1)S(1)} %slice.128), channel_id=1, source_target_pairs={{31,0},{28,1},{29,2},{30,3},{3,4},{0,5},{1,6},{2,7},{7,8},{4,9},{5... | collective-permute-start | bytes 98312 | tf_op jit(solution)/shard_map/cond/branch_2_fun/ppermute | solution.py:339
  34.7 6.3 %collective-permute-start.43 = (bf16[64,512]{1,0:T(8,128)(2,1)S(1)}, bf16[64,512]{1,0:T(8,128)(2,1)S(1)}, u32[]{:S(2)}, u32[]{:S(2)}) collective-permute-start(bf16[64,512]{1,0:T(8,128)(2,1)S(1)} %slice.127), channel_id=1, source_target_pairs={{3,0},{0,1},{1,2},{2,3},{7,4},{4,5},{5,6},{6,7},{11,8},{8,9},{9,10... | collective-permute-start | bytes 196616 | tf_op jit(solution)/shard_map/cond/branch_2_fun/ppermute | solution.py:338
  35.2 5.8 %collective-permute-start.42 = (bf16[64,512]{1,0:T(8,128)(2,1)S(1)}, bf16[64,512]{1,0:T(8,128)(2,1)S(1)}, u32[]{:S(2)}, u32[]{:S(2)}) collective-permute-start(bf16[64,512]{1,0:T(8,128)(2,1)S(1)} %slice.126), channel_id=1, source_target_pairs={{28,0},{0,4},{4,8},{8,12},{12,16},{16,20},{20,24},{24,28},{29,1},{... | collective-permute-start | bytes 196616 | tf_op jit(solution)/shard_map/cond/branch_2_fun/ppermute | solution.py:340

commit v4 on v3

--- a/solution.py
+++ b/solution.py
@@ -459,7 +459,7 @@
 
 def before_coarse(flags, fine, table, weight, plan):
     own, width = fine.shape
-    half = 3 * weight.shape[0] // 8
+    half = 5 * weight.shape[0] // 16
 
     def body(flags_ref, rows_ref, fine_ref, weight_hbm, x_ref, part_hbm, home_ref, weight_ref, part_ref, sems):
         start = Copies(sems)
@@ -494,8 +494,9 @@
     count, width = x_own.shape
     inner = w_proj.shape[0]
 
-    def body(own_ref, source_ref, ids_ref, qkv_w_ref, proj_w_ref, rows_ref, out_ref, *refs):
-        *piece_outs, x_ref, qkv_ref, id_ref, _ = refs
+    def body(own_ref, source_ref, ids_ref, qkv_w_ref, proj_w_hbm, rows_ref, out_ref, *refs):
+        *piece_outs, x_ref, qkv_ref, id_ref, proj_w_ref, sems = refs
+        proj_w = Copies(sems)(proj_w_hbm, proj_w_ref)
         id_ref[...] = id_columns(ids_ref[: -(-count // 128), :], count)
         take = columns_of(rows_of(plan, rows_ref, "take_one"), count) - float(count)
         x = own_ref[...].astype(F32) + select_rows(take, source_ref[...])
@@ -508,6 +509,7 @@
             out = jnp.dot(out, proj_w_ref[...], preferred_element_type=F32)
             out_ref[at, :] = (x_ref[at, :] + out).astype(BF16)
 
+        proj_w.wait()
         attend_windows(
             lambda w, at: qkv_ref[w * TOK : (w + 1) * TOK, at : at + 128],
             lambda w: id_ref[w * TOK : (w + 1) * TOK, :],
@@ -523,9 +525,10 @@
         pltpu.VMEM((count, width), F32),
         pltpu.VMEM((count, 3 * inner), BF16),
         pltpu.VMEM((count, 128), BF16),
+        pltpu.VMEM(w_proj.shape, BF16),
     ]
     args = [x_own, source, ids, w_qkv, w_proj, rows]
-    out, *sent = call(body, outs, args, [VMEM] * len(args), scratch, 1, 3 << 30, 6 << 20, 14)
+    out, *sent = call(body, outs, args, [VMEM] * 4 + [HBM, VMEM], scratch, 1, 3 << 30, 6 << 20, 14)
     return out, sent
 
 
@@ -702,9 +705,9 @@
 
     sent, source, table, flags, one, two, three = first_pieces(shifts, tokens, plan)
     got, (ids, x, weights) = choose(
-        one, branches(first, plan.one_branches), sent, flags, regions, source, table, [fine_qkv, fine_proj]
+        one, branches(first, plan.one_branches), sent, flags, regions, source, table, [fine_qkv]
     )
-    fine, sent = fine_level(x, got, ids, *weights, table, plan)
+    fine, sent = fine_level(x, got, ids, *weights, fine_proj, table, plan)
     got, (x, part, home, merge_first) = choose(
         two, branches(second, plan.two_branches), sent, flags, fine, table, merge_weight
     )

time: 42 us -> 42 us (level); the launches traced: 42.5 us -> 41.8 us
  local copies, waits for them, and re-layouts: 2.92 us -> 0.04 us
  starting transfers between devices: 11.3 us -> 14 us
  waiting for transfers between devices: 7.76 us -> 6.38 us
  Pallas kernels: 19 us -> 19.9 us
    ppermute x3, starting transfers between devices: 5.87 us -> 8.32 us  [exchange(): both = lax.ppermute(both, ('lat', 'lon'), pairs)]
    unnamed x4 -> x0, local copies, waits for them, and re-layouts: 2.1 us -> none
    ppermute x3, waiting for transfers between devices: 6.39 us -> 5.13 us  [exchange(): both = lax.ppermute(both, ('lat', 'lon'), pairs)]
    pallas_call x9, Pallas kernels: 19 us -> 19.9 us  [call(): pl.pallas_call(body, out_shape=outs, in_specs=in_specs, out_specs=out_spe...]
    cond x4 -> x0, local copies, waits for them, and re-layouts: 0.79 us -> none
  transfers between devices with their start and end apart: 9 -> 9, of which waited for: 5 -> 3; matrix products, arithmetic and copies ran while one was open for 0% -> 0% of each run, Pallas kernels for 13% -> 14%
where the time goes in v4:
time: 42 us; the launch traced here: 41.8 us
  Pallas kernels  19.9 us (47%)
  starting transfers between devices  14 us (33%)
  waiting for transfers between devices  6.38 us (15%)
  between operations  0.85 us (2%)
  loops' own time  0.61 us (1%)
    pallas_call x9, Pallas kernels, call(): pl.pallas_call(body, out_shape=outs, in_specs=in_specs, out_specs=out_spe...  19.9 us
    ppermute x3, starting transfers between devices, exchange(): both = lax.ppermute(both, ('lat', 'lon'), pairs)  8.32 us
    ppermute x3, waiting for transfers between devices, exchange(): both = lax.ppermute(both, ('lat', 'lon'), pairs)  5.13 us
    ppermute x3, starting transfers between devices, exchange(): col = lax.ppermute(col, 'lon', [((j + sign) % lon, j) for j in range(lon)])  4.37 us
    ppermute x3, starting transfers between devices, exchange(): row = lax.ppermute(row, 'lat', [((i + sign) % lat, i) for i in range(lat)])  1.28 us
    ppermute x3, waiting for transfers between devices, exchange(): col = lax.ppermute(col, 'lon', [((j + sign) % lon, j) for j in range(lon)])  1.24 us
  transfers between devices with their start and end apart: 9, of which 3 were waited for; matrix products, arithmetic and copies ran while one was open for 0% of the time, Pallas kernels for 14%

profile of v4, /device:TPU:0, one launch (start us, length us, event | category | flops | bytes accessed | tf_op | source)
XLA Modules:
  0.0 41.8 jit_solution(12746096392614854066)
XLA Ops:
  0.6 1.6 %shard_map.116 = (bf16[112,512]{1,0:T(8,128)(2,1)S(1)}, bf16[112,512]{1,0:T(8,128)(2,1)S(1)}, bf16[48,512]{1,0:T(8,128)(2,1)S(1)}, bf16[576,512]{1,0:T(8,128)(2,...) custom-call(s32[2]{0:T(128)} %shifts_hbm.1, ...), custom_call_target="tpu_custom_call" | custom-call | flops 268435456 | bytes 1048576 | tf_op jit(solution)/shard_map/pallas_call | solution.py:275
  2.2 11.6 %conditional.3 = (bf16[272,512]{1,0:T(8,128)(2,1)S(1)}, f32[7,128]{1,0:T(8,128)S(1)}, bf16[576,512]{1,0:T(8,128)(2,1)S(1)}, bf16[512,1536]{1,0:T(8,128)(2,1)S(1)}) conditional(s32[]{:T(128)S(4)} %bitcast.13, (bf16[112,512]{1,0:T(8,128)(2,1)S(1)}, bf16[112,512]{1,0:T(8,128)(2,1)S(1)}, bf16[48,512]{1,0:T(8,128)(2,1)S(1)}, ...), branch_computations={%region_0.0_spmd, %region_1.0_spmd, %region_2.0_spmd, %region_3.0_... | conditional | flops 268435456 | bytes 5619864 | solution.py:356
  2.3 0.5 %collective-permute-start.12 = (bf16[112,512]{1,0:T(8,128)(2,1)S(1)}, bf16[112,512]{1,0:T(8,128)(2,1)S(1)}, u32[]{:S(2)}, u32[]{:S(2)}) collective-permute-start(bf16[112,512]{1,0:T(8,128)(2,1)S(1)} %get-tuple-element.306), channel_id=1, source_target_pairs={{28,0},{0,4},{4,8},{8,12},{12,16},{16,20},{20,24},{24,28},{29,1},{... | collective-permute-start | bytes 344072 | tf_op jit(solution)/shard_map/cond/branch_4_fun/ppermute | solution.py:340
  2.8 2.6 %collective-permute-start.13 = (bf16[112,512]{1,0:T(8,128)(2,1)S(1)}, bf16[112,512]{1,0:T(8,128)(2,1)S(1)}, u32[]{:S(2)}, u32[]{:S(2)}) collective-permute-start(bf16[112,512]{1,0:T(8,128)(2,1)S(1)} %get-tuple-element.307), channel_id=1, source_target_pairs={{3,0},{0,1},{1,2},{2,3},{7,4},{4,5},{5,6},{6,7},{11,8},{8,9},{9,10... | collective-permute-start | bytes 344072 | tf_op jit(solution)/shard_map/cond/branch_4_fun/ppermute | solution.py:338
  5.4 2.4 %collective-permute-start.14 = (bf16[40,512]{1,0:T(8,128)(2,1)S(1)}, bf16[40,512]{1,0:T(8,128)(2,1)S(1)}, u32[]{:S(2)}, u32[]{:S(2)}) collective-permute-start(bf16[40,512]{1,0:T(8,128)(2,1)S(1)} %slice.102), channel_id=1, source_target_pairs={{31,0},{28,1},{29,2},{30,3},{3,4},{0,5},{1,6},{2,7},{7,8},{4,9},{5... | collective-permute-start | bytes 122888 | tf_op jit(solution)/shard_map/cond/branch_4_fun/ppermute | solution.py:339
  7.8 1.7 %branch_4_fun.7 = (f32[7,128]{1,0:T(8,128)S(1)}, bf16[576,512]{1,0:T(8,128)(2,1)S(1)}, bf16[512,1536]{1,0:T(8,128)(2,1)S(1)}) custom-call(s32[8]{0:T(128)S(4)} %get-tuple-element.309.flags_ref, f32[32,128]{1,0:T(8,128)S(1)} %get-tuple-element.310.rows_ref, bf16[576,512]{1,0:T(8,128)(2,1)S(1)} %get-tuple-element.311.tokens_ref, s32[192,96]{1,0:T(8,128)} %bitcast.18, ...), custom_call_target="tpu_custom_call" | custom-call | flops 268435456 | bytes 4194304 | tf_op jit(solution)/shard_map/cond/branch_4_fun/pallas_call | solution.py:275
  9.5 4.2 %collective-permute-done.14.refs_2_ = bf16[40,512]{1,0:T(8,128)(2,1)S(1)} collective-permute-done((bf16[40,512]{1,0:T(8,128)(2,1)S(1)}, bf16[40,512]{1,0:T(8,128)(2,1)S(1)}, u32[]{:S(2)}, u32[]{:S(2)}) %collective-permute-start.14) | collective-permute-done | bytes 40992 | tf_op jit(solution)/shard_map/cond/branch_4_fun/ppermute | solution.py:339
  13.7 0.0 collective-permute-done.12.refs_0_
  13.7 0.0 collective-permute-done.13.refs_1_
  13.8 6.4 %shard_map.117 = (bf16[576,512]{1,0:T(8,128)(2,1)S(1)}, bf16[160,512]{1,0:T(8,128)(2,1)S(1)}, bf16[160,512]{1,0:T(8,128)(2,1)S(1)}, bf16[112,512]{1,0:T(8,128)(2,1)S(1)}) custom-call(bf16[576,512]{1,0:T(8,128)(2,1)S(1)} %get-tuple-element.479.own_ref, bf16[272,512]{1,0:T(8,128)(2,1)S(1)} %get-tuple-element.480.source_ref, ...), custom_call_target="tpu_custom_call" | custom-call | flops 3221225472 | bytes 6291456 | tf_op jit(solution)/shard_map/pallas_call | solution.py:275
  20.2 5.9 %conditional.4 = (bf16[432,512]{1,0:T(8,128)(2,1)S(1)}, bf16[576,512]{1,0:T(8,128)(2,1)S(1)}, bf16[576,512]{1,0:T(8,128)(2,1)}, bf16[112,512]{1,0:T(8,128)(2,1)S(1)}, bf16[640,1024]{1,0:T(8,128)(2,1)S(1)}) conditional(s32[]{:T(128)S(4)} %bitcast.12, (bf16[160,512]{1,0:T(8,128)(2,1)S(1)}, ...), branch_computations={%region_5.0_spmd, %region_6.0_spmd, %region_7.0_spmd, %region_8.0_... | conditional | flops 268435456 | bytes 6619296 | solution.py:356
  20.4 1.7 %collective-permute-start.25 = (bf16[120,512]{1,0:T(8,128)(2,1)S(1)}, bf16[120,512]{1,0:T(8,128)(2,1)S(1)}, u32[]{:S(2)}, u32[]{:S(2)}) collective-permute-start(bf16[120,512]{1,0:T(8,128)(2,1)S(1)} %slice.113), channel_id=1, source_target_pairs={{1,0},{2,1},{3,2},{0,3},{5,4},{6,5},{7,6},{4,7},{9,8},{10,9},{11,1... | collective-permute-start | bytes 368648 | tf_op jit(solution)/shard_map/cond/branch_3_fun/ppermute | solution.py:338
  22.2 0.4 %collective-permute-start.24 = (bf16[120,512]{1,0:T(8,128)(2,1)S(1)}, bf16[120,512]{1,0:T(8,128)(2,1)S(1)}, u32[]{:S(2)}, u32[]{:S(2)}) collective-permute-start(bf16[120,512]{1,0:T(8,128)(2,1)S(1)} %slice.112), channel_id=1, source_target_pairs={{4,0},{8,4},{12,8},{16,12},{20,16},{24,20},{28,24},{0,28},{5,1},{9... | collective-permute-start | bytes 368648 | tf_op jit(solution)/shard_map/cond/branch_3_fun/ppermute | solution.py:340
  22.6 0.9 %collective-permute-start.26 = (bf16[40,512]{1,0:T(8,128)(2,1)S(1)}, bf16[40,512]{1,0:T(8,128)(2,1)S(1)}, u32[]{:S(2)}, u32[]{:S(2)}) collective-permute-start(bf16[40,512]{1,0:T(8,128)(2,1)S(1)} %slice.114), channel_id=1, source_target_pairs={{5,0},{6,1},{7,2},{4,3},{9,4},{10,5},{11,6},{8,7},{13,8},{14,9},{1... | collective-permute-start | bytes 122888 | tf_op jit(solution)/shard_map/cond/branch_3_fun/ppermute | solution.py:339
  23.5 1.6 %branch_3_fun.9 = (bf16[576,512]{1,0:T(8,128)(2,1)S(1)}, bf16[576,512]{1,0:T(8,128)(2,1)}, bf16[112,512]{1,0:T(8,128)(2,1)S(1)}, bf16[640,1024]{1,0:T(8,128)(2,1)S(1)}) custom-call(s32[8]{0:T(128)S(4)} %get-tuple-element.353.flags_ref, f32[32,128]{1,0:T(8,128)S(1)} %get-tuple-element.354.rows_ref, bf16[576,512]{1,0:T(8,128)(2,1)S(1)} %get-tuple-element.355.fine_ref, ...), custom_call_target="tpu_custom_call" | custom-call | flops 268435456 | bytes 4194304 | tf_op jit(solution)/shard_map/cond/branch_3_fun/pallas_call | solution.py:275
  25.1 1.0 %collective-permute-done.26.refs_2_ = bf16[40,512]{1,0:T(8,128)(2,1)S(1)} collective-permute-done((bf16[40,512]{1,0:T(8,128)(2,1)S(1)}, bf16[40,512]{1,0:T(8,128)(2,1)S(1)}, u32[]{:S(2)}, u32[]{:S(2)}) %collective-permute-start.26) | collective-permute-done | bytes 40992 | tf_op jit(solution)/shard_map/cond/branch_3_fun/ppermute | solution.py:339
  26.0 0.0 collective-permute-done.25.refs_1_
  26.0 0.0 collective-permute-done.24.refs_0_
  26.1 5.1 %shard_map.118 = (bf16[144,1024]{1,0:T(8,128)(2,1)S(1)}, bf16[128,512]{1,0:T(8,128)(2,1)S(1)}, bf16[128,512]{1,0:T(8,128)(2,1)S(1)}, bf16[88,512]{1,0:T(8,128)(2,1)S(1)}) custom-call(s32[8]{0:T(128)S(4)} %get-tuple-element.476.flags_ref, bf16[2048,1024]{1,0:T(8,128)(2,1)} %merge_hbm.1, bf16[1024,1536]{1,0:T(8,128)(2,1)} %qkv_w_hbm.1, ...), custom_call_target="tpu_custom_call" | custom-call | flops 3221225472 | bytes 12582912 | tf_op jit(solution)/shard_map/pallas_call | solution.py:275
  31.2 10.4 %conditional.5 = (bf16[2,12,24,512]{3,2,1,0:T(8,128)(2,1)}, bf16[2,6,12,1024]{3,0,2,1:T(2,128)(2,1)}) conditional(s32[]{:T(128)S(4)} %bitcast.11, (bf16[576,512]{1,0:T(8,128)(2,1)}, bf16[432,512]{1,0:T(8,128)(2,1)S(1)}, f32[32,128]{1,0:T(8,128)S(1)}, bf16[128,512]{1,0:T(8,128)(2,1)S(1)}, ...), branch_computations={%region_12.0_spmd, %region_13.0_spmd, %region_14.0_spmd, %region_1... | conditional | flops 1342177280 | bytes 6865032 | solution.py:356
  31.2 5.0 %collective-permute-start.41 = (bf16[16,512]{1,0:T(8,128)(2,1)S(1)}, bf16[16,512]{1,0:T(8,128)(2,1)S(1)}, u32[]{:S(2)}, u32[]{:S(2)}) collective-permute-start(bf16[16,512]{1,0:T(8,128)(2,1)S(1)} %slice.125), channel_id=1, source_target_pairs={{5,0},{6,1},{7,2},{4,3},{9,4},{10,5},{11,6},{8,7},{13,8},{14,9},{1... | collective-permute-start | bytes 49160 | tf_op jit(solution)/shard_map/cond/branch_1_fun/ppermute | solution.py:339
  36.2 0.0 collective-permute-start.40
  36.2 0.4 collective-permute-start.39
  36.5 2.5 %branch_1_fun.10 = bf16[2,12,24,512]{3,2,1,0:T(8,128)(2,1)} custom-call(bf16[576,512]{1,0:T(8,128)(2,1)} %get-tuple-element.401.part_hbm, bf16[432,512]{1,0:T(8,128)(2,1)S(1)} %get-tuple-element.402.source_ref, f32[32,128]{1,0:T(8,128)S(1)} %get-tuple-element.403.rows_ref.refs_3_), custom_call_target="tpu_custom_call" | custom-call | flops 1073741824 | bytes 4194304 | tf_op jit(solution)/shard_map/cond/branch_1_fun/pallas_call | solution.py:275
  39.0 0.0 collective-permute-done.41.refs_2_
  39.0 1.2 %collective-permute-done.40.refs_1_ = bf16[48,512]{1,0:T(8,128)(2,1)S(1)} collective-permute-done((bf16[48,512]{1,0:T(8,128)(2,1)S(1)}, bf16[48,512]{1,0:T(8,128)(2,1)S(1)}, u32[]{:S(2)}, u32[]{:S(2)}) %collective-permute-start.40) | collective-permute-done | bytes 49184 | tf_op jit(solution)/shard_map/cond/branch_1_fun/ppermute | solution.py:338
  40.3 0.0 collective-permute-done.39.refs_0_
  40.3 1.1 %branch_1_fun.11 = bf16[6,12,2,1024]{3,2,1,0:T(2,128)(2,1)} custom-call(bf16[144,1024]{1,0:T(8,128)(2,1)S(1)} %get-tuple-element.404.coarse_ref, bf16[48,512]{1,0:T(8,128)(2,1)S(1)} %collective-permute-done.39.refs_0_, bf16[48,512]{1,0:T(8,128)(2,1)S(1)} %collective-permute-done.40.refs_1_, bf16[16,512]{1,0:T(8,128)(2,1)S(1)} %collective-permute-done.41.refs_2_, ...), custom_call_target="tpu_custom_call" | custom-call | flops 268435456 | bytes 1048576 | tf_op jit(solution)/shard_map/cond/branch_1_fun/pallas_call | solution.py:275
  (9 shorter events, 0.1 us)
Async XLA Ops:
  2.3 11.5 %collective-permute-start.12 = (bf16[112,512]{1,0:T(8,128)(2,1)S(1)}, bf16[112,512]{1,0:T(8,128)(2,1)S(1)}, u32[]{:S(2)}, u32[]{:S(2)}) collective-permute-start(bf16[112,512]{1,0:T(8,128)(2,1)S(1)} %get-tuple-element.306), channel_id=1, source_target_pairs={{28,0},{0,4},{4,8},{8,12},{12,16},{16,20},{20,24},{24,28},{29,1},{... | collective-permute-start | bytes 344072 | tf_op jit(solution)/shard_map/cond/branch_4_fun/ppermute | solution.py:340
  2.8 11.0 %collective-permute-start.13 = (bf16[112,512]{1,0:T(8,128)(2,1)S(1)}, bf16[112,512]{1,0:T(8,128)(2,1)S(1)}, u32[]{:S(2)}, u32[]{:S(2)}) collective-permute-start(bf16[112,512]{1,0:T(8,128)(2,1)S(1)} %get-tuple-element.307), channel_id=1, source_target_pairs={{3,0},{0,1},{1,2},{2,3},{7,4},{4,5},{5,6},{6,7},{11,8},{8,9},{9,10... | collective-permute-start | bytes 344072 | tf_op jit(solution)/shard_map/cond/branch_4_fun/ppermute | solution.py:338
  5.4 8.3 %collective-permute-start.14 = (bf16[40,512]{1,0:T(8,128)(2,1)S(1)}, bf16[40,512]{1,0:T(8,128)(2,1)S(1)}, u32[]{:S(2)}, u32[]{:S(2)}) collective-permute-start(bf16[40,512]{1,0:T(8,128)(2,1)S(1)} %slice.102), channel_id=1, source_target_pairs={{31,0},{28,1},{29,2},{30,3},{3,4},{0,5},{1,6},{2,7},{7,8},{4,9},{5... | collective-permute-start | bytes 122888 | tf_op jit(solution)/shard_map/cond/branch_4_fun/ppermute | solution.py:339
  20.4 5.6 %collective-permute-start.25 = (bf16[120,512]{1,0:T(8,128)(2,1)S(1)}, bf16[120,512]{1,0:T(8,128)(2,1)S(1)}, u32[]{:S(2)}, u32[]{:S(2)}) collective-permute-start(bf16[120,512]{1,0:T(8,128)(2,1)S(1)} %slice.113), channel_id=1, source_target_pairs={{1,0},{2,1},{3,2},{0,3},{5,4},{6,5},{7,6},{4,7},{9,8},{10,9},{11,1... | collective-permute-start | bytes 368648 | tf_op jit(solution)/shard_map/cond/branch_3_fun/ppermute | solution.py:338
  22.2 3.9 %collective-permute-start.24 = (bf16[120,512]{1,0:T(8,128)(2,1)S(1)}, bf16[120,512]{1,0:T(8,128)(2,1)S(1)}, u32[]{:S(2)}, u32[]{:S(2)}) collective-permute-start(bf16[120,512]{1,0:T(8,128)(2,1)S(1)} %slice.112), channel_id=1, source_target_pairs={{4,0},{8,4},{12,8},{16,12},{20,16},{24,20},{28,24},{0,28},{5,1},{9... | collective-permute-start | bytes 368648 | tf_op jit(solution)/shard_map/cond/branch_3_fun/ppermute | solution.py:340
  22.6 3.4 %collective-permute-start.26 = (bf16[40,512]{1,0:T(8,128)(2,1)S(1)}, bf16[40,512]{1,0:T(8,128)(2,1)S(1)}, u32[]{:S(2)}, u32[]{:S(2)}) collective-permute-start(bf16[40,512]{1,0:T(8,128)(2,1)S(1)} %slice.114), channel_id=1, source_target_pairs={{5,0},{6,1},{7,2},{4,3},{9,4},{10,5},{11,6},{8,7},{13,8},{14,9},{1... | collective-permute-start | bytes 122888 | tf_op jit(solution)/shard_map/cond/branch_3_fun/ppermute | solution.py:339
  31.2 7.8 %collective-permute-start.41 = (bf16[16,512]{1,0:T(8,128)(2,1)S(1)}, bf16[16,512]{1,0:T(8,128)(2,1)S(1)}, u32[]{:S(2)}, u32[]{:S(2)}) collective-permute-start(bf16[16,512]{1,0:T(8,128)(2,1)S(1)} %slice.125), channel_id=1, source_target_pairs={{5,0},{6,1},{7,2},{4,3},{9,4},{10,5},{11,6},{8,7},{13,8},{14,9},{1... | collective-permute-start | bytes 49160 | tf_op jit(solution)/shard_map/cond/branch_1_fun/ppermute | solution.py:339
  36.2 4.1 %collective-permute-start.40 = (bf16[48,512]{1,0:T(8,128)(2,1)S(1)}, bf16[48,512]{1,0:T(8,128)(2,1)S(1)}, u32[]{:S(2)}, u32[]{:S(2)}) collective-permute-start(bf16[48,512]{1,0:T(8,128)(2,1)S(1)} %slice.124), channel_id=1, source_target_pairs={{1,0},{2,1},{3,2},{0,3},{5,4},{6,5},{7,6},{4,7},{9,8},{10,9},{11,1... | collective-permute-start | bytes 147464 | tf_op jit(solution)/shard_map/cond/branch_1_fun/ppermute | solution.py:338
  36.2 4.1 %collective-permute-start.39 = (bf16[48,512]{1,0:T(8,128)(2,1)S(1)}, bf16[48,512]{1,0:T(8,128)(2,1)S(1)}, u32[]{:S(2)}, u32[]{:S(2)}) collective-permute-start(bf16[48,512]{1,0:T(8,128)(2,1)S(1)} %slice.123), channel_id=1, source_target_pairs={{4,0},{8,4},{12,8},{16,12},{20,16},{24,20},{28,24},{0,28},{5,1},{9... | collective-permute-start | bytes 147464 | tf_op jit(solution)/shard_map/cond/branch_1_fun/ppermute | solution.py:340
